TPU v7x, 256 devices: a whole 4x4x8 slice. The times are simulated.
256 devices in a mesh: sample: 4 (over y), space: 64 (over z, x, core).
Axes of the slice: x: 4, y: 4, z: 8, core: 2. Of those that a mesh axis runs over, the one named last changes fastest.
Arguments:
- volumes: bfloat16 [4, 4, 512, 32, 256], P(None, None, 'space', 'sample'), may hold values from -6 to 6
- weight_one: bfloat16 [16, 4, 3, 3, 3], replicated, may hold values from -0.625 to 0.625
- weight_two: bfloat16 [32, 16, 3, 3, 3], replicated, may hold values from -0.3125 to 0.3125
- weight_three: bfloat16 [64, 32, 3, 3, 3], replicated, may hold values from -0.21875 to 0.21875
- feature_grad: bfloat16 [4, 64, 64, 128], P('sample', None, 'space'), may hold values from -6 to 6
Outputs:
- features: bfloat16 [4, 64, 64, 128], P('sample', None, 'space')
- grad_act_one: bfloat16 [4, 16, 256, 16, 128], P(None, None, 'space', 'sample')
- wgrad_one: float32 [16, 4, 3, 3, 3], replicated
- wgrad_two: float32 [32, 16, 3, 3, 3], replicated
- wgrad_three: float32 [64, 32, 3, 3, 3], replicated
All inputs are finite; a program needn't handle non-finite values.
Results may differ from a plain program's by a relative error of at most 0.023.
Values may be sent and summed in bfloat16 or wider, within the bound.
A program may use at most 192 MiB of HBM per device.

v0:
```python
import math

import jax
import jax.numpy as jnp
from jax import lax
from jax.sharding import PartitionSpec as P

LAYOUT = ("NCDHW", "OIDHW", "NCDHW")
FILTER_LAYOUT = ("CNDHW", "IODHW", "CNDHW")
GRAD_GAIN = 4.0


def shifted(block, axis, distance):
    devices = range(lax.axis_size(axis))
    route = [(i - distance, i) for i in devices if i - distance in devices]
    return lax.ppermute(block, axis, route)


def strided_conv(padded, weights, paddings):
    return lax.conv_general_dilated(
        padded,
        weights,
        (2, 2, 2),
        paddings,
        dimension_numbers=LAYOUT,
        preferred_element_type=jnp.float32,
    )


def spread_conv(gradient, weights, paddings):
    flipped = jnp.flip(jnp.swapaxes(weights, 0, 1), (2, 3, 4))
    return lax.conv_general_dilated(
        gradient,
        flipped,
        (1, 1, 1),
        paddings,
        lhs_dilation=(2, 2, 2),
        dimension_numbers=LAYOUT,
        preferred_element_type=jnp.float32,
    )


def filter_grad(padded, gradient, paddings):
    return lax.conv_general_dilated(
        padded,
        gradient,
        (1, 1, 1),
        paddings,
        rhs_dilation=(2, 2, 2),
        dimension_numbers=FILTER_LAYOUT,
        preferred_element_type=jnp.float32,
    )


def activate(pre_act):
    root = jnp.sqrt(pre_act * pre_act + 1.0)
    active = (0.65 * pre_act + 0.35 * (root - 1.0)).astype(jnp.bfloat16)
    slope = (0.65 + 0.35 * pre_act / root).astype(jnp.bfloat16)
    return (active, slope)


def with_next_plane(volume_in):
    next_face = shifted(volume_in[:, :, :1], "space", -1)
    return jnp.concatenate([volume_in, next_face], axis=2)


def with_next_block(volume_in):
    widened = with_next_plane(volume_in)
    edge_row = shifted(widened[:, :, :, :1], "sample", -1)
    return jnp.concatenate([widened, edge_row], axis=3)


def spread_back(gradient, weights, with_rows):
    row_pads = (2, 2) if with_rows else (2, 1)
    spread = spread_conv(gradient, weights, ((2, 2), row_pads, (2, 1)))
    if with_rows:
        back_row = shifted(spread[:, :, :, -1:].astype(jnp.bfloat16), "sample", 1).astype(
            jnp.float32
        )
        spread = jnp.concatenate([spread[:, :, :, :1] + back_row, spread[:, :, :, 1:-1]], axis=3)
    back_face = shifted(spread[:, :, -1:].astype(jnp.bfloat16), "space", 1).astype(jnp.float32)
    return jnp.concatenate([spread[:, :, :1] + back_face, spread[:, :, 1:-1]], axis=2)


def local(volumes, weight_one, weight_two, weight_three, feature_grad):
    samples = volumes.shape[0]
    total_x = volumes.shape[2] * lax.axis_size("space")
    total_y = volumes.shape[3] * lax.axis_size("sample")
    total_z = volumes.shape[4]
    block_pads = ((0, 0), (0, 0), (0, 1))
    slab_pads = ((0, 0), (0, 1), (0, 1))
    input_one = with_next_block(volumes)
    act_one, slope_one = activate(strided_conv(input_one, weight_one, block_pads))
    input_two = with_next_block(act_one)
    act_two, slope_two = activate(strided_conv(input_two, weight_two, block_pads))
    regrouped = lax.all_to_all(act_two, "sample", split_axis=0, concat_axis=3, tiled=True)
    input_three = with_next_plane(regrouped)
    act_three, slope_three = activate(strided_conv(input_three, weight_three, slab_pads))
    features = act_three.reshape(feature_grad.shape)
    grad_three = (
        feature_grad.reshape(act_three.shape).astype(jnp.float32) * slope_three.astype(jnp.float32)
    ).astype(jnp.bfloat16)
    down_two = spread_back(grad_three, weight_three, False).astype(jnp.bfloat16)
    returned = lax.all_to_all(down_two, "sample", split_axis=3, concat_axis=0, tiled=True)
    grad_two = (returned.astype(jnp.float32) * slope_two.astype(jnp.float32)).astype(jnp.bfloat16)
    down_one = spread_back(grad_two, weight_two, True)
    grad_act_one = down_one.astype(jnp.bfloat16)
    grad_one = (down_one * slope_one.astype(jnp.float32)).astype(jnp.bfloat16)
    summed = lax.psum(
        (
            filter_grad(input_one, grad_one, block_pads),
            filter_grad(input_two, grad_two, block_pads),
            filter_grad(input_three, grad_three, slab_pads),
        ),
        ("sample", "space"),
    )
    scale_one = GRAD_GAIN / math.sqrt(samples * (total_x // 2) * (total_y // 2) * (total_z // 2))
    scale_two = GRAD_GAIN / math.sqrt(samples * (total_x // 4) * (total_y // 4) * (total_z // 4))
    scale_three = GRAD_GAIN / math.sqrt(samples * (total_x // 8) * (total_y // 8) * (total_z // 8))
    return (
        features,
        grad_act_one,
        summed[0] * scale_one,
        summed[1] * scale_two,
        summed[2] * scale_three,
    )


def solution(mesh):
    in_specs = (
        P(None, None, "space", "sample", None),
        P(),
        P(),
        P(),
        P("sample", None, "space", None),
    )
    out_specs = (
        P("sample", None, "space", None),
        P(None, None, "space", "sample", None),
        P(),
        P(),
        P(),
    )
    return jax.shard_map(local, mesh=mesh, in_specs=in_specs, out_specs=out_specs, check_vma=False)
```

profile of v0, /device:TPU:1, one launch (start us, length us, event | category | flops | bytes accessed | tf_op | source)
XLA Modules:
  0.0 561.4 jit_solution(14456995260843853936)
XLA Ops:
  8.1 5.1 collective-permute-start
  16.0 14.0 %copy.162 = bf16[4,4,9,8,256]{0,1,4,3,2:T(4,128)(2,1)} copy(bf16[4,4,9,8,256]{4,3,2,1,0:T(8,128)(2,1)S(1)} %constant_dynamic-update-slice_fusion) | data formatting | bytes 1179648 | tf_op jit(solution)/shard_map/concatenate | solution.py:64
  30.0 2.5 copy.163
  32.6 16.3 %fusion.2 = bf16[4,9,9,4,256]{3,0,4,2,1:T(4,128)(2,1)} fusion(bf16[4,4,9,1,256]{0,1,4,3,2:T(4,128)(2,1)S(1)} %copy.163, bf16[4,4,9,8,256]{0,1,4,3,2:T(4,128)(2,1)} %copy.162), kind=kLoop, calls=%fused_computation.4 | loop fusion | flops 331776 | bytes 1327104 | tf_op jit(solution)/shard_map/concatenate | solution.py:70
  48.9 16.2 %pad = bf16[4,9,9,4,272]{3,0,4,2,1:T(4,128)(2,1)} pad(bf16[4,9,9,4,256]{3,0,4,2,1:T(4,128)(2,1)} %fusion.2, bf16[]{:T(256)} %constant.24), padding=0_0x0_0x0_0x0_0x0_16 | pad | bytes 1368578 | tf_op jit(solution)/shard_map/concatenate | solution.py:70
  65.1 37.3 %copy.165 = bf16[4,9,9,4,8,34]{5,4,3,2,1,0:T(8,128)(2,1)S(1)} copy(bf16[4,9,9,4,8,34]{3,0,5,4,2,1:T(4,128)(2,1)} %bitcast.138) | data formatting | bytes 1410048 | tf_op jit(solution)/shard_map/conv_general_dilated | solution.py:20
  103.2 3.3 fusion.7
  106.5 6.5 %copy.166 = bf16[4,9,9,32,36]{3,0,4,2,1:T(4,128)(2,1)S(1)} copy(bf16[4,9,9,32,36]{4,3,2,1,0:T(8,128)(2,1)} %fusion.7) | data formatting | bytes 1492992 | tf_op jit(solution)/shard_map/conv_general_dilated | solution.py:20
  113.0 5.4 fusion.9
  118.4 3.4 copy.167
  127.5 3.6 collective-permute-done.2
  132.7 4.3 collective-permute-done.3
  138.8 3.8 reshape.70
  144.1 3.4 fusion.5
  147.6 5.1 copy.173
  152.7 2.3 fusion.23
  155.8 8.6 %all_to_all.27 = bf16[4,2,4096]{2,1,0:T(2,128)(2,1)S(1)} all-to-all(bf16[4,2,4096]{2,1,0:T(2,128)(2,1)S(1)} %reshape.140), channel_id=1, replica_groups=mesh['sample'=4,'space'=64] {'sample'}, dimensions={0} | all-to-all | bytes 131072 | tf_op jit(solution)/shard_map/all_to_all | solution.py:96
  167.5 3.4 copy.204
  170.9 4.4 reshape.111
  176.1 3.6 copy.206
  183.1 2.4 fusion.37
  186.4 4.6 collective-permute-start.5
  194.0 3.5 all-to-all-start.1
  198.2 3.7 all-to-all-done.1
  203.6 6.3 %convolution_select_fusion = f32[5,5,32,18,16]{2,4,3,1,0:T(8,128)S(1)} fusion(bf16[32,16,3,3,3]{0,1,4,3,2:T(8,128)(2,1)S(1)} %copy-done.9, pred[32,18]{0,1:T(8,128)(4,1)S(1)} %copy-done.10, bf16[32,2,2,4,8,10]{0,3,5,4,2,1:T(4,128)(2,1)S(1)} %fusion.20), kind=kOutput, calls=%fused_computation.14 | convolution fusion | flops 32080896 | bytes 1031744 | tf_op jit(solution)/shard_map/conv_general_dilated | solution.py:32
  215.2 3.0 copy.202
  218.2 3.4 reshape.109
  221.6 5.0 fusion.58
  227.8 6.2 %collective-permute-start.7 = (bf16[4,16,1,4,128]{4,0,1,3,2:T(4,128)(2,1)S(1)}, bf16[4,16,1,4,128]{4,0,1,3,2:T(4,128)(2,1)S(1)}, u32[]{:S(2)}, u32[]{:S(2)}) collective-permute-start(bf16[4,16,1,4,128]{4,0,1,3,2:T(4,128)(2,1)S(1)} %fusion.33), channel_id=1, source_target_pairs={{0,1},{1,2},{2,3},{3,4},{4,5},{5,6},{6,7},{7,8},{8,9},{9,10},{10,1... | collective-permute-start | bytes 196616 | tf_op jit(solution)/shard_map/ppermute | solution.py:16
  234.0 208.1 %all-reduce.3.cloned.1.call-done = f32[64,32,3,3,3]{0,1,4,3,2:T(8,128)} async-done(((f32[64,32,3,3,3]{0,1,4,3,2:T(8,128)}), f32[64,32,3,3,3]{0,1,4,3,2:T(8,128)}) %all-reduce.3.cloned.1.call-update) | async-done | bytes 221200 | tf_op jit(solution)/shard_map/psum | solution.py:109
  445.7 27.0 %fusion.1 = f32[16,4,3,3,3]{0,1,4,3,2:T(4,128)S(1)} fusion(bf16[4,16,4,4,128]{1,0,4,3,2:T(4,128)(2,1)S(1)} %copy.205, bf16[4,4,9,1,256]{0,1,4,3,2:T(4,128)(2,1)} %copy-done.2, bf16[4,4,9,8,256]{0,1,4,3,2:T(4,128)(2,1)} %copy.162), kind=kOutput, calls=%fused_computation.3 | convolution fusion | flops 29564928 | bytes 932608 | tf_op jit(solution)/shard_map/conv_general_dilated | solution.py:44
  472.7 79.1 %all-reduce = (f32[16,4,3,3,3]{0,1,4,3,2:T(4,128)S(1)}, f32[32,16,3,3,3]{0,1,4,3,2:T(8,128)S(1)}) all-reduce(f32[16,4,3,3,3]{0,1,4,3,2:T(4,128)S(1)} %fusion.1, f32[32,16,3,3,3]{0,1,4,3,2:T(8,128)S(1)} %fusion.58), channel_id=1, replica_groups=mesh['sample'=4,'space'=64] {'sample','space'}, use_global_device_ids=true, to_apply=%region_0.1 | all-reduce | flops 15552 | bytes 124416 | tf_op jit(solution)/shard_map/psum | solution.py:109
  (136 shorter events, 40.8 us)
Async XLA Ops:
  7.2 175.1 %copy-start = (bf16[64,32,3,3,3]{0,1,4,3,2:T(8,128)(2,1)S(1)}, bf16[64,32,3,3,3]{0,1,4,3,2:T(8,128)(2,1)}, u32[]{:S(2)}) copy-start(bf16[64,32,3,3,3]{0,1,4,3,2:T(8,128)(2,1)} %param.8) | copy-start | bytes 331780
  7.2 435.0 %all-reduce.3.cloned.1.call-start = ((), (), s32[]{:S(2)}) async-start(), calls=%async_computation.2 | async-start | bytes 884736 | tf_op jit(solution)/shard_map/psum | solution.py:109
  8.1 6.4 %collective-permute-start = (bf16[4,4,1,8,256]{4,3,2,1,0:T(8,128)(2,1)S(1)}, bf16[4,4,1,8,256]{4,3,2,1,0:T(8,128)(2,1)S(1)}, u32[]{:S(2)}, u32[]{:S(2)}) collective-permute-start(bf16[4,4,1,8,256]{4,3,2,1,0:T(8,128)(2,1)S(1)} %slice.46), channel_id=1, source_target_pairs={{1,0},{2,1},{3,2},{4,3},{5,4},{6,5},{7,6},{8,7},{9,8},{10,9},{11,1... | collective-permute-start | bytes 196616 | tf_op jit(solution)/shard_map/ppermute | solution.py:16
  14.7 15.3 %collective-permute-start.1 = (bf16[4,4,9,1,256]{4,1,3,2,0:T(4,128)(2,1)S(1)}, bf16[4,4,9,1,256]{4,1,3,2,0:T(4,128)(2,1)S(1)}, u32[]{:S(2)}, u32[]{:S(2)}) collective-permute-start(bf16[4,4,9,1,256]{4,1,3,2,0:T(4,128)(2,1)S(1)} %copy.211), channel_id=1, source_target_pairs={{64,0},{128,64},{192,128},{65,1},{129,65},{193,129},{66,2},{130,66... | collective-permute-start | bytes 221192 | tf_op jit(solution)/shard_map/ppermute | solution.py:16
  32.6 16.3 %copy-start.2 = (bf16[4,4,9,1,256]{0,1,4,3,2:T(4,128)(2,1)}, bf16[4,4,9,1,256]{0,1,4,3,2:T(4,128)(2,1)S(1)}, u32[]{:S(2)}) copy-start(bf16[4,4,9,1,256]{0,1,4,3,2:T(4,128)(2,1)S(1)} %copy.163) | copy-start | bytes 221188
  106.5 6.5 %copy-start.13 = (bf16[16,4,3,3,3]{0,1,4,3,2:T(4,128)(2,1)S(1)}, bf16[16,4,3,3,3]{0,1,4,3,2:T(4,128)(2,1)}, u32[]{:S(2)}) copy-start(bf16[16,4,3,3,3]{0,1,4,3,2:T(4,128)(2,1)} %param.6) | copy-start | bytes 10372
  106.5 6.5 %copy-start.14 = (pred[32,17]{0,1:T(8,128)(4,1)S(1)}, pred[32,17]{0,1:T(8,128)(4,1)}, u32[]{:S(2)}) copy-start(pred[32,17]{0,1:T(8,128)(4,1)} %constant.46) | copy-start | bytes 1636
  125.6 5.6 collective-permute-start.2
  131.2 5.8 %collective-permute-start.3 = (bf16[4,16,5,1,128]{4,1,3,2,0:T(8,128)(2,1)S(1)}, bf16[4,16,5,1,128]{4,1,3,2,0:T(8,128)(2,1)S(1)}, u32[]{:S(2)}, u32[]{:S(2)}) collective-permute-start(bf16[4,16,5,1,128]{4,1,3,2,0:T(8,128)(2,1)S(1)} %slice.90), channel_id=1, source_target_pairs={{64,0},{128,64},{192,128},{65,1},{129,65},{193,129},{66,2},{130,66... | collective-permute-start | bytes 245768 | tf_op jit(solution)/shard_map/ppermute | solution.py:16
  147.6 5.1 copy-start.8
  147.6 5.2 copy-start.15
  155.1 12.3 %copy-start.11 = (bf16[1,64,1,128]{3,1,2,0:T(8,128)(2,1)S(1)}, bf16[1,64,1,128]{3,1,2,0:T(8,128)(2,1)}, u32[]{:S(2)}) copy-start(bf16[1,64,1,128]{3,1,2,0:T(8,128)(2,1)} %param.9) | copy-start | bytes 49156
  155.1 12.4 %copy-start.4 = (f32[4,4,32,17,16]{2,4,3,1,0:T(8,128)S(1)}, f32[4,4,32,17,16]{2,4,3,1,0:T(8,128)}, u32[]{:S(2)}) copy-start(f32[4,4,32,17,16]{2,4,3,1,0:T(8,128)} %get-tuple-element.27) | copy-start | bytes 1671172
  165.3 14.4 %collective-permute-start.4 = (bf16[1,32,1,8,64]{1,0,4,3,2:T(2,128)(2,1)S(1)}, bf16[1,32,1,8,64]{1,0,4,3,2:T(2,128)(2,1)S(1)}, u32[]{:S(2)}, u32[]{:S(2)}) collective-permute-start(bf16[1,32,1,8,64]{1,0,4,3,2:T(2,128)(2,1)S(1)} %slice.93), channel_id=1, source_target_pairs={{1,0},{2,1},{3,2},{4,3},{5,4},{6,5},{7,6},{8,7},{9,8},{10,9},{11,1... | collective-permute-start | bytes 98312 | tf_op jit(solution)/shard_map/ppermute | solution.py:16
  170.9 4.4 copy-start.6
  170.9 5.1 copy-start.5
  179.7 2.6 copy-start.16
  183.1 2.6 copy-start.12
  186.4 6.5 %collective-permute-start.5 = (bf16[1,32,1,8,64]{1,3,4,0,2:T(8,128)(2,1)S(1)}, bf16[1,32,1,8,64]{1,3,4,0,2:T(8,128)(2,1)S(1)}, u32[]{:S(2)}, u32[]{:S(2)}) collective-permute-start(bf16[1,32,1,8,64]{1,3,4,0,2:T(8,128)(2,1)S(1)} %slice_bitcast_fusion.7), channel_id=1, source_target_pairs={{0,1},{1,2},{2,3},{3,4},{4,5},{5,6},{6,7},{7,8},{8,9},{9,10},{10,1... | collective-permute-start | bytes 98312 | tf_op jit(solution)/shard_map/ppermute | solution.py:16
  191.0 12.5 %copy-start.9 = (bf16[32,16,3,3,3]{0,1,4,3,2:T(8,128)(2,1)S(1)}, bf16[32,16,3,3,3]{0,1,4,3,2:T(8,128)(2,1)}, u32[]{:S(2)}) copy-start(bf16[32,16,3,3,3]{0,1,4,3,2:T(8,128)(2,1)} %param.7) | copy-start | bytes 82948
  191.1 12.5 %copy-start.10 = (pred[32,18]{0,1:T(8,128)(4,1)S(1)}, pred[32,18]{0,1:T(8,128)(4,1)}, u32[]{:S(2)}) copy-start(pred[32,18]{0,1:T(8,128)(4,1)} %constant.47) | copy-start | bytes 1732
  194.0 7.9 %all-to-all-start.1 = ((bf16[4,2,4096]{2,1,0:T(2,128)(2,1)}), bf16[4,2,4096]{2,1,0:T(2,128)(2,1)S(1)}, u32[]{:S(2)}, u32[]{:S(2)}) async-start(bf16[4,2,4096]{2,1,0:T(2,128)(2,1)} %reshape.142), calls=%async_computation.1 | async-start | bytes 131072 | tf_op jit(solution)/shard_map/all_to_all | solution.py:104
  209.9 1.8 copy-start.1
  213.0 14.8 %collective-permute-start.6 = (bf16[4,16,5,1,128]{4,0,1,2,3:T(4,128)(2,1)S(1)}, bf16[4,16,5,1,128]{4,0,1,2,3:T(4,128)(2,1)S(1)}, u32[]{:S(2)}, u32[]{:S(2)}) collective-permute-start(bf16[4,16,5,1,128]{4,0,1,2,3:T(4,128)(2,1)S(1)} %slice_bitcast_fusion.8), channel_id=1, source_target_pairs={{0,64},{64,128},{128,192},{1,65},{65,129},{129,193},{2,66},{66,130... | collective-permute-start | bytes 245768 | tf_op jit(solution)/shard_map/ppermute | solution.py:16
  218.2 3.4 copy-start.7
  221.6 5.1 slice-start
  227.7 216.4 %copy-start.3 = (f32[4,4,4,136,16]{3,2,4,1,0:T(4,128)S(1)}, f32[4,4,4,136,16]{3,2,4,1,0:T(4,128)}, u32[]{:S(2)}) copy-start(f32[4,4,4,136,16]{3,2,4,1,0:T(4,128)} %reshape.111) | copy-start | bytes 1671172
  227.8 216.1 %collective-permute-start.7 = (bf16[4,16,1,4,128]{4,0,1,3,2:T(4,128)(2,1)S(1)}, bf16[4,16,1,4,128]{4,0,1,3,2:T(4,128)(2,1)S(1)}, u32[]{:S(2)}, u32[]{:S(2)}) collective-permute-start(bf16[4,16,1,4,128]{4,0,1,3,2:T(4,128)(2,1)S(1)} %fusion.33), channel_id=1, source_target_pairs={{0,1},{1,2},{2,3},{3,4},{4,5},{5,6},{6,7},{7,8},{8,9},{9,10},{10,1... | collective-permute-start | bytes 196616 | tf_op jit(solution)/shard_map/ppermute | solution.py:16
Sparse Core Ops, SparseCore 0:
  185.7 256.4 all-reduce.2
where the time goes:
time: 571 us; the launch traced here: 561 us
  waiting for transfers between devices  222 us (39%)
  local copies, waits for them, and re-layouts  129 us (23%)
  blocking collectives  87.7 us (15%)
  matrix products  49.9 us (9%)
  other arithmetic  29.2 us (5%)
  starting transfers between devices  28.3 us (5%)
  between operations  15.3 us (3%)
    psum x1, waiting for transfers between devices, local(): lax.psum((filter_grad(input_one, grad_one, block_pads), filter_grad(input...  208 us
    psum x1, blocking collectives, local(): lax.psum((filter_grad(input_one, grad_one, block_pads), filter_grad(input...  79.1 us
    conv_general_dilated x8, local copies, waits for them, and re-layouts, strided_conv(): lax.conv_general_dilated(padded, weights, (2, 2, 2), paddings, dimension_...  54.6 us
    conv_general_dilated x3, matrix products, filter_grad(): lax.conv_general_dilated(padded, gradient, (1, 1, 1), paddings, rhs_dilat...  34.5 us
    ppermute x8, starting transfers between devices, shifted(): return lax.ppermute(block, axis, route)  24.8 us
    concatenate x3, local copies, waits for them, and re-layouts, with_next_block(): return jnp.concatenate([widened, edge_row], axis=3)  20.8 us
    concatenate x2, other arithmetic, with_next_block(): return jnp.concatenate([widened, edge_row], axis=3)  17.1 us
    concatenate x5, local copies, waits for them, and re-layouts, with_next_plane(): return jnp.concatenate([volume_in, next_face], axis=2)  14.7 us
  transfers between devices with their start and end apart: 10, of which 6 were waited for; matrix products, arithmetic and copies ran while one was open for 10% of the time, Pallas kernels for 0%

commit v1 on v0

v1 whole, which is shorter than its diff:
```python
import math

import jax
import jax.numpy as jnp
import ml_dtypes
import numpy as np
from jax import lax
from jax.experimental import pallas as pl
from jax.experimental.pallas import tpu as pltpu
from jax.sharding import PartitionSpec as P

GRAD_GAIN = 4.0
MESH = pl.DeviceIdType.MESH
F32 = jnp.float32
BF16 = jnp.bfloat16
TAPS_THREE = {-1: (1, 2), 0: (0, 1)}
TAPS_TWO = {-1: (2,), 0: (0, 1, 2), 1: (0, 1)}
COPIES = 128


def every_second(blocks, cells):
    half = cells // 2
    out = np.zeros((blocks, cells, 3, blocks, half), np.float32)
    for b in range(blocks):
        for f in range(3):
            for k in range(half):
                if 2 * k + f < cells:
                    out[b, 2 * k + f, f, b, k] = 1
    return out.reshape(blocks * cells, 3 * blocks * half)


def row_orders():
    main = np.zeros((8, 8, 16, 3, 4, 8, 8), np.float32)
    halo = np.zeros((17, 16, 3, 80), np.float32)
    edge = np.zeros((80, 4, 8, 8), np.float32)
    pads = np.zeros((9, 16, 9, 12), np.float32)
    cells = np.zeros((16, 4, 4, 4, 4, 16), np.float32)
    for c in range(4):
        for x in range(8):
            for y in range(8):
                for f in range(3):
                    main[x, y, f * 4 + c, f, c, x, y] = 1
        for u in range(8):
            edge[c * 8 + u, c, 0, u] = 1
            edge[32 + c * 8 + u, c, u, 0] = 1
            for f in range(3):
                halo[u, f * 4 + c, f, c * 8 + u] = 1
                halo[9 + u, f * 4 + c, f, 32 + c * 8 + u] = 1
        edge[64 + c, c, 0, 0] = 1
        for f in range(3):
            halo[8, f * 4 + c, f, 64 + c] = 1
    for t in range(9):
        for r in range(12):
            pads[t, r, t, r] = 1
    for c in range(16):
        for x in range(4):
            for y in range(4):
                cells[c, x, y, x, y, c] = 1
    return (
        main.reshape(1024, 768),
        halo.reshape(272, 240),
        edge.reshape(80, 256),
        pads.reshape(144, 108),
        cells.reshape(256, 256),
    )


def mm(a, b):
    return jnp.dot(a, b, preferred_element_type=F32)


def mm_t(a, b):
    return lax.dot_general(a, b, (((1,), (1,)), ((), ())), preferred_element_type=F32)


def activate(p):
    square = p * p + 1.0
    inverse = lax.rsqrt(square)
    active = (0.65 * p + 0.35 * (square * inverse - 1.0)).astype(BF16)
    slope = (0.65 + 0.35 * (p * inverse)).astype(BF16)
    return active, slope


def identity(n):
    return (
        lax.broadcasted_iota(jnp.int32, (n, n), 0) == lax.broadcasted_iota(jnp.int32, (n, n), 1)
    ).astype(F32).astype(BF16)


def make_kernel(ny, ns, gx, scales):
    gz = ns // gx
    rows3 = 128 // gx

    def kernel(vol, w1t, w2t, w3t, fg, s1, s2, s3, pm, ph, pq, pw, po, feat, gact, o1, o2, o3,
               w1, w2, w3, w2k, w3k, hs, hr, vsm, vsh, e1, a1, sl1, e2, a2, sl2, e3, fgs, fts,
               g3, gg3, g2e, gg2, d1b, wb3, r3, p3, q3, z3, f3, wb2, y2, p2, q2, z2, f2,
               y1, x1, z1, ss, rs):
        y = lax.axis_index("sample")
        s = lax.axis_index("space")
        gx_me = lax.rem(s, gx)
        gz_me = lax.div(s, gx)
        y_prev, y_next = lax.rem(y + ny - 1, ny), lax.rem(y + 1, ny)
        s_prev, s_next = lax.rem(s + ns - 1, ns), lax.rem(s + 1, ns)
        y_peers = [{"sample": lax.rem(y + d, ny), "space": s} for d in range(1, ny)]
        x_peers = [{"sample": y, "space": gz_me * gx + lax.rem(gx_me + d, gx)} for d in range(1, gx)]
        z_peers = [{"sample": y, "space": lax.rem(s + d * gx, ns)} for d in range(1, gz)]
        prev = [
            {"sample": y, "space": s_prev},
            {"sample": y_prev, "space": s},
            {"sample": y_prev, "space": s_prev},
        ]
        following = [
            {"sample": y, "space": s_next},
            {"sample": y_next, "space": s},
            {"sample": y_next, "space": s_next},
        ]
        started = []

        def send(src, dst, device):
            n = len(started)
            copy = pltpu.make_async_remote_copy(
                src_ref=src, dst_ref=dst, send_sem=ss.at[n], recv_sem=rs.at[n],
                device_id=device, device_id_type=MESH,
            )
            copy.start()
            started.append(copy)
            return copy

        def arrive(copies):
            for copy in copies:
                copy.wait_recv()

        barrier = pltpu.get_barrier_semaphore()
        greeted = y_peers + x_peers + z_peers + [prev[0], prev[2], following[0], following[2]]
        for device in greeted:
            pl.semaphore_signal(barrier, inc=1, device_id=device, device_id_type=MESH)

        more_x = jnp.where(s == ns - 1, 0.0, 1.0).astype(F32)
        more_y = jnp.where(y == ny - 1, 0.0, 1.0).astype(F32)
        less_x = jnp.where(s == 0, 0.0, 1.0).astype(F32)
        less_y = jnp.where(y == 0, 0.0, 1.0).astype(F32)

        for b in range(4):
            hs[b] = mm(pq[...], vol[b]).astype(BF16)
        fgs[y] = fg[...]
        pl.semaphore_wait(barrier, len(greeted))
        spans = ((0, 32), (32, 32), (64, 16))
        got_vol = [
            send(hs.at[:, pl.ds(at, n)], hr.at[:, pl.ds(at, n)], prev[i])
            for i, (at, n) in enumerate(spans)
        ]
        got_fg = [send(fgs.at[y], fgs.at[y], device) for device in y_peers]

        w1pad = mm(pw[...], w1t[...]).astype(BF16)
        w1[...] = mm_t(identity(16), w1pad).astype(BF16)
        w2[...] = mm_t(identity(32), w2t[...]).astype(BF16)
        w3[...] = mm_t(identity(64), w3t[...]).astype(BF16)
        w2rows = w2t[...].reshape(9, 3, 16, 32)
        w3rows = w3t[...].reshape(9, 3, 32, 64)
        for f in range(3):
            w2k[:, f * 32:(f + 1) * 32] = w2rows[:, f].reshape(144, 32)
            w3k[:, f * 64:(f + 1) * 64] = w3rows[:, f].reshape(288, 64)

        for b in range(4):
            part = mm(vol[b], s1[...]).astype(BF16)
            for f in range(3):
                vsm[f * 256:(f + 1) * 256, b * 128:(b + 1) * 128] = part[:, f * 128:(f + 1) * 128]
        for x in range(8):
            block = mm(pm[x * 128:(x + 1) * 128, :], vsm[...]).astype(BF16)
            e1[x * 9:x * 9 + 8] = block.reshape(8, 16, 512)

        arrive(got_vol)
        row = lax.broadcasted_iota(jnp.int32, (80, 384), 0)
        inside = jnp.where(row < 32, more_x, jnp.where(row < 64, more_y, more_x * more_y))
        for b in range(4):
            part = (mm(hr[b], s1[...]) * inside).astype(BF16)
            for f in range(3):
                vsh[f * 80:(f + 1) * 80, b * 128:(b + 1) * 128] = part[:, f * 128:(f + 1) * 128]
        block = mm(ph[...], vsh[...]).astype(BF16).reshape(17, 16, 512)
        e1[72:81] = block[:9]
        for x in range(8):
            e1[x * 9 + 8] = block[9 + x]

        def columns_one(i, j):
            return jnp.concatenate(
                [e1[(2 * i + a) * 9 + 2 * j:(2 * i + a) * 9 + 2 * j + 3].reshape(48, 512) for a in range(3)],
                axis=0,
            )

        def cell_one(i, j):
            act, slope = activate(mm(w1[...], columns_one(i, j)))
            a1[i * 5 + j] = act
            sl1[i * 4 + j] = slope

        for j in range(4):
            cell_one(0, j)
        got_act = [
            send(a1.at[pl.ds(0, 4)], a1.at[pl.ds(20, 4)], prev[0]),
            send(a1.at[0], a1.at[24], prev[2]),
        ]
        got_rows = [send(a1.at[0], a1.at[4], prev[1])]
        for i in range(1, 4):
            for j in range(4):
                cell_one(i, j)
                if j == 0:
                    got_rows.append(send(a1.at[i * 5], a1.at[i * 5 + 4], prev[1]))

        def widen_two(cells, rows, keep):
            for p in range(2):
                part = mm(rows[:, p * 256:(p + 1) * 256], s2[...])
                if keep is not None:
                    part = part * keep
                part = part.astype(BF16).reshape(len(cells), 16, 384)
                for n, cell in enumerate(cells):
                    for f in range(3):
                        e2[cell, f * 16:(f + 1) * 16, p * 128:(p + 1) * 128] = part[n, :, f * 128:(f + 1) * 128]

        for x in range(4):
            widen_two([x * 5 + k for k in range(4)], a1[x * 5:x * 5 + 4].reshape(64, 512), None)
        arrive(got_act + got_rows)
        far = [20, 21, 22, 23, 24, 4, 9, 14, 19]
        row = lax.broadcasted_iota(jnp.int32, (144, 384), 0)
        inside = jnp.where(row < 64, more_x, jnp.where(row < 80, more_x * more_y, more_y))
        widen_two(far, jnp.concatenate([a1[cell] for cell in far], axis=0), inside)

        def columns_two(i, j):
            return jnp.concatenate(
                [e2[(2 * i + a) * 5 + 2 * j:(2 * i + a) * 5 + 2 * j + 3].reshape(144, 256) for a in range(3)],
                axis=0,
            )

        for i in range(2):
            for j in range(2):
                act, slope = activate(mm(w2[...], columns_two(i, j)))
                a2[i * 3 + j] = act
                sl2[(i + 1) * 3 + j + 1] = slope
        got_act = [
            send(a2.at[pl.ds(0, 2)], a2.at[pl.ds(6, 2)], prev[0]),
            send(a2.at[0], a2.at[2], prev[1]),
            send(a2.at[3], a2.at[5], prev[1]),
            send(a2.at[0], a2.at[8], prev[2]),
        ]
        got_slope = [
            send(sl2.at[pl.ds(7, 2)], sl2.at[pl.ds(1, 2)], following[0]),
            send(sl2.at[5], sl2.at[3], following[1]),
            send(sl2.at[8], sl2.at[6], following[1]),
            send(sl2.at[8], sl2.at[0], following[2]),
        ]

        def widen_three(cells, rows, keep):
            part = mm(rows, s3[...])
            if keep is not None:
                part = part * keep
            part = part.astype(BF16).reshape(len(cells), 32, 384)
            for n, cell in enumerate(cells):
                for f in range(3):
                    e3[cell, f * 32:(f + 1) * 32, :] = part[n, :, f * 128:(f + 1) * 128]

        near = [0, 1, 3, 4]
        widen_three(near, jnp.concatenate([a2[cell] for cell in near], axis=0), None)
        row = lax.broadcasted_iota(jnp.int32, (512, 128), 0)
        lane = lax.broadcasted_iota(jnp.int32, (512, 128), 1)
        source = lax.div(lane, 32) * 128 + y * 32 + lax.rem(lane, 32)
        regroup = (row == source).astype(F32).astype(BF16)
        arrive(got_fg)
        cotangent = mm(jnp.concatenate([fgs[k] for k in range(4)], axis=1), regroup)
        arrive(got_act)
        far = [6, 7, 8, 2, 5]
        row = lax.broadcasted_iota(jnp.int32, (160, 384), 0)
        inside = jnp.where(row < 64, more_x, jnp.where(row < 96, more_x * more_y, more_y))
        widen_three(far, jnp.concatenate([a2[cell] for cell in far], axis=0), inside)
        act, slope = activate(mm(w3[...], e3[...].reshape(864, 128)))
        grad_three = (cotangent * slope.astype(F32)).astype(BF16)
        g3[3] = grad_three
        fts[y] = act
        got_grad = [send(g3.at[3], g3.at[to], following[i]) for i, to in enumerate((1, 2, 0))]
        got_feat = [send(fts.at[y], fts.at[y], device) for device in y_peers]

        part = mm_t(e3[...].reshape(864, 128), grad_three)
        wb3[...] = jnp.zeros_like(wb3)
        for n in range(27):
            group, at = divmod(n * 16, rows3)
            for half in range(2):
                wb3[group // gx, group % gx, at:at + 16, half * 64:(half + 1) * 64] = (
                    part[half * 432 + n * 16:half * 432 + (n + 1) * 16]
                )
        got_r3 = [
            send(wb3.at[device["sample"]], r3.at[d], device) for d, device in enumerate(y_peers)
        ]

        arrive(got_grad)
        row = lax.broadcasted_iota(jnp.int32, (256, 128), 0)
        inside = jnp.where(
            row < 64, less_x * less_y, jnp.where(row < 128, less_x, jnp.where(row < 192, less_y, 1.0))
        )
        rows = (g3[...].reshape(256, 128).astype(F32) * inside).astype(BF16)
        for f in range(3):
            part = mm_t(rows, s3[:, f * 128:(f + 1) * 128]).astype(BF16)
            gg3[:, f * 64:(f + 1) * 64, :] = part.reshape(4, 64, 256)
        down = {}
        for i in (-1, 0):
            for j in (-1, 0):
                picked = jnp.concatenate(
                    [w3k[(a * 3 + e) * 32:(a * 3 + e + 1) * 32, :] for a in TAPS_THREE[i] for e in TAPS_THREE[j]],
                    axis=0,
                )
                part = mm(picked, gg3[(i + 1) * 2 + j + 1])
                n = 0
                for a in TAPS_THREE[i]:
                    for e in TAPS_THREE[j]:
                        key = (2 * i + a, 2 * j + e)
                        term = part[n * 32:(n + 1) * 32]
                        down[key] = term if key not in down else down[key] + term
                        n += 1
        arrive(got_slope)
        for i in range(-1, 2):
            for j in range(-1, 2):
                cell = (i + 1) * 3 + j + 1
                rounded = down[i, j].astype(BF16).astype(F32)
                g2e[cell] = (rounded * sl2[cell].astype(F32)).astype(BF16)

        part = None
        for i in range(2):
            for j in range(2):
                term = mm_t(columns_two(i, j), g2e[(i + 1) * 3 + j + 1])
                part = term if part is None else part + term
        wb2[...] = jnp.zeros_like(wb2)
        for n in range(27):
            lanes, at = divmod(n * 16, 112)
            wb2[at:at + 16, lanes * 32:(lanes + 1) * 32] = part[n * 16:(n + 1) * 16]
        y2[y] = wb2[...]
        got_y2 = [send(y2.at[y], y2.at[y], device) for device in y_peers]

        arrive(got_r3)
        p3[...] = (wb3[y] + r3[0]) + (r3[1] + r3[2])
        got_q3 = [
            send(p3.at[lax.rem(gx_me + d + 1, gx)], q3.at[d], device) for d, device in enumerate(x_peers)
        ]

        for p in range(2):
            rows = g2e[...].reshape(288, 256)[:, p * 128:(p + 1) * 128]
            for f in range(3):
                part = mm_t(rows, s2[:, f * 128:(f + 1) * 128]).astype(BF16)
                gg2[:, f * 32:(f + 1) * 32, p * 256:(p + 1) * 256] = part.reshape(9, 32, 256)
        down = {}
        for i in (-1, 0, 1):
            for j in (-1, 0, 1):
                picked = jnp.concatenate(
                    [w2k[(a * 3 + e) * 16:(a * 3 + e + 1) * 16, :] for a in TAPS_TWO[i] for e in TAPS_TWO[j]],
                    axis=0,
                )
                part = mm(picked, gg2[(i + 1) * 3 + j + 1])
                n = 0
                for a in TAPS_TWO[i]:
                    for e in TAPS_TWO[j]:
                        key = (2 * i + a, 2 * j + e)
                        term = part[n * 16:(n + 1) * 16]
                        down[key] = term if key not in down else down[key] + term
                        n += 1

        part = None
        for i in range(4):
            for j in range(4):
                d1b[(i * 4 + j) * 16:(i * 4 + j + 1) * 16, :] = down[i, j].astype(BF16)
                grad_one = (down[i, j] * sl1[i * 4 + j].astype(F32)).astype(BF16)
                term = mm_t(columns_one(i, j), grad_one)
                part = term if part is None else part + term
        y1[y, :, 0:144] = part.T
        y1[y, :, 144:256] = jnp.zeros((16, 112), F32)
        got_y1 = [send(y1.at[y], y1.at[y], device) for device in y_peers]

        arrive(got_y2)
        total = (y2[0] + y2[1]) + (y2[2] + y2[3])
        for t in range(gx):
            p2[t] = total[t * rows3:(t + 1) * rows3]
        got_q2 = [
            send(p2.at[lax.rem(gx_me + d + 1, gx)], q2.at[d], device) for d, device in enumerate(x_peers)
        ]
        arrive(got_q3)
        total = p3[gx_me]
        for d in range(gx - 1):
            total = total + q3[d]
        z3[gz_me] = total
        got_z3 = [send(z3.at[gz_me], z3.at[gz_me], device) for device in z_peers]

        block = mm(po[...], d1b[...]).astype(BF16)
        for b in range(4):
            gact[b] = block[:, b * 128:(b + 1) * 128]
        arrive(got_feat)
        feat[...] = mm(jnp.concatenate([fts[k] for k in range(4)], axis=1), regroup).astype(BF16)

        arrive(got_y1)
        x1[gx_me] = (y1[0] + y1[1]) + (y1[2] + y1[3])
        got_x1 = [send(x1.at[gx_me], x1.at[gx_me], device) for device in x_peers]
        arrive(got_q2)
        total = p2[gx_me]
        for d in range(gx - 1):
            total = total + q2[d]
        z2[gz_me] = total
        got_z2 = [send(z2.at[gz_me], z2.at[gz_me], device) for device in z_peers]
        arrive(got_z3)
        total = z3[0]
        for d in range(1, gz):
            total = total + z3[d]
        f3[y, gx_me] = total * scales[2]
        got_f3 = [send(f3.at[y, gx_me], f3.at[y, gx_me], device) for device in x_peers]

        arrive(got_x1)
        total = x1[0]
        for d in range(1, gx):
            total = total + x1[d]
        z1[gz_me] = total
        got_z1 = [send(z1.at[gz_me], z1.at[gz_me], device) for device in z_peers]
        arrive(got_z2)
        total = z2[0]
        for d in range(1, gz):
            total = total + z2[d]
        f2[gx_me] = total * scales[1]
        got_f2 = [send(f2.at[gx_me], f2.at[gx_me], device) for device in x_peers]
        arrive(got_f3)
        got_last = [send(f3.at[y], f3.at[y], device) for device in y_peers]

        arrive(got_z1)
        total = z1[0]
        for d in range(1, gz):
            total = total + z1[d]
        total = (total * scales[0]).T
        for t in range(9):
            o1[t * 12:(t + 1) * 12, :] = total[t * 16:t * 16 + 12]
        arrive(got_f2)
        total = f2[...].reshape(128, 128)
        for n in range(27):
            lanes, at = divmod(n * 16, 112)
            o2[n * 16:(n + 1) * 16, :] = total[at:at + 16, lanes * 32:(lanes + 1) * 32]
        arrive(got_last)
        total = f3[...].reshape(512, 128)[:432]
        for half in range(2):
            o3[half * 432:(half + 1) * 432, :] = total[:, half * 64:(half + 1) * 64]
        for copy in started:
            copy.wait_send()

    vm = pltpu.VMEM
    scratch = [
        vm((16, 144), BF16), vm((32, 432), BF16), vm((64, 864), BF16), vm((144, 96), BF16), vm((288, 192), BF16),
        vm((4, 80, 256), BF16), vm((4, 80, 256), BF16), vm((768, 512), BF16), vm((240, 512), BF16),
        vm((81, 16, 512), BF16), vm((25, 16, 512), BF16), vm((16, 16, 512), BF16), vm((25, 48, 256), BF16),
        vm((9, 32, 256), BF16), vm((9, 32, 256), BF16), vm((9, 96, 128), BF16),
        vm((4, 64, 128), BF16), vm((4, 64, 128), BF16), vm((4, 64, 128), BF16), vm((4, 192, 256), BF16),
        vm((9, 32, 256), BF16), vm((9, 96, 512), BF16), vm((256, 512), BF16),
        vm((ny, gx, rows3, 128), F32), vm((ny - 1, gx, rows3, 128), F32), vm((gx, rows3, 128), F32),
        vm((gx - 1, rows3, 128), F32), vm((gz, rows3, 128), F32), vm((ny, gx, rows3, 128), F32),
        vm((128, 128), F32), vm((ny, 128, 128), F32), vm((gx, rows3, 128), F32), vm((gx - 1, rows3, 128), F32),
        vm((gz, rows3, 128), F32), vm((gx, rows3, 128), F32),
        vm((ny, 16, 256), F32), vm((gx, 16, 256), F32), vm((gz, 16, 256), F32),
        pltpu.SemaphoreType.DMA((COPIES,)), pltpu.SemaphoreType.DMA((COPIES,)),
    ]
    return pl.pallas_call(
        kernel,
        out_shape=(
            jax.ShapeDtypeStruct((64, 128), BF16),
            jax.ShapeDtypeStruct((4, 256, 128), BF16),
            jax.ShapeDtypeStruct((108, 16), F32),
            jax.ShapeDtypeStruct((432, 32), F32),
            jax.ShapeDtypeStruct((864, 64), F32),
        ),
        in_specs=[pl.BlockSpec(memory_space=pltpu.VMEM)] * 13,
        out_specs=[pl.BlockSpec(memory_space=pltpu.VMEM)] * 5,
        scratch_shapes=scratch,
        compiler_params=pltpu.CompilerParams(
            collective_id=0, has_side_effects=True, vmem_limit_bytes=48 * 1024 * 1024
        ),
        cost_estimate=pl.CostEstimate(flops=6_000_000_000, bytes_accessed=8_000_000, transcendentals=0),
        name="layers",
    )


def solution(mesh):
    ny, ns = mesh.shape["sample"], mesh.shape["space"]
    gx = 8 if ns % 8 == 0 and ns > 8 else 2
    select = [every_second(1, 256), every_second(2, 128), every_second(4, 64)]
    consts = [np.asarray(c).astype(ml_dtypes.bfloat16) for c in select + list(row_orders())]

    def local(volumes, weight_one, weight_two, weight_three, feature_grad):
        cells = volumes.shape[0] * volumes.shape[2] * ns * volumes.shape[3] * ny * volumes.shape[4]
        scales = [GRAD_GAIN / math.sqrt(cells // 8**n) for n in (1, 2, 3)]
        flat = [
            jnp.transpose(w, (2, 3, 4, 1, 0)).reshape(-1, w.shape[0])
            for w in (weight_one, weight_two, weight_three)
        ]
        features, grad_act, one, two, three = make_kernel(ny, ns, gx, scales)(
            volumes.reshape(4, 256, 256), *flat, feature_grad.reshape(64, 128), *consts
        )

        def filters(array, channels):
            return jnp.transpose(array.reshape(3, 3, 3, channels, -1), (4, 3, 0, 1, 2))

        return (
            features.reshape(feature_grad.shape),
            grad_act.reshape(4, 16, 4, 4, 128),
            filters(one, 4),
            filters(two, 16),
            filters(three, 32),
        )

    in_specs = (
        P(None, None, "space", "sample", None),
        P(),
        P(),
        P(),
        P("sample", None, "space", None),
    )
    out_specs = (
        P("sample", None, "space", None),
        P(None, None, "space", "sample", None),
        P(),
        P(),
        P(),
    )
    return jax.shard_map(local, mesh=mesh, in_specs=in_specs, out_specs=out_specs, check_vma=False)
```

time: 571 us -> 66.5 us (0.12); the launches traced: 561 us -> 65.8 us
  waiting for transfers between devices: 222 us -> 0 us
  local copies, waits for them, and re-layouts: 129 us -> 15.3 us
  blocking collectives: 87.7 us -> 0 us
  matrix products: 49.9 us -> 0 us
  Pallas kernels: 0 us -> 49.8 us
  other arithmetic: 29.2 us -> 0 us
  starting transfers between devices: 28.3 us -> 0 us
  between operations: 15.3 us -> 0.66 us
    psum x1 -> x0, waiting for transfers between devices: 208 us -> none  [local(): lax.psum((filter_grad(input_one, grad_one, block_pads), filter_grad(input...]
    psum x1 -> x0, blocking collectives: 79.1 us -> none  [local(): lax.psum((filter_grad(input_one, grad_one, block_pads), filter_grad(input...]
    conv_general_dilated x20 -> x0, local copies, waits for them, and re-layouts: 62.3 us -> none  [the longest x8 54.6 us: strided_conv(): lax.conv_general_dilated(padded, weights, (2, 2, 2), paddings, dimension_...]
    conv_general_dilated x8 -> x0, matrix products: 49.9 us -> none  [the longest x3 34.5 us: filter_grad(): lax.conv_general_dilated(padded, gradient, (1, 1, 1), paddings, rhs_dilat...]
    pallas_call x0 -> x1, Pallas kernels: none -> 49.8 us  [local(): make_kernel(ny, ns, gx, scales)]
    concatenate x9 -> x0, local copies, waits for them, and re-layouts: 35.7 us -> none  [the longest x3 20.8 us: with_next_block(): return jnp.concatenate([widened, edge_row], axis=3)]
    ppermute x8 -> x0, starting transfers between devices: 24.8 us -> none  [shifted(): return lax.ppermute(block, axis, route)]
    concatenate x4 -> x0, other arithmetic: 18.6 us -> none  [the longest x2 17.1 us: with_next_block(): return jnp.concatenate([widened, edge_row], axis=3)]
  transfers between devices with their start and end apart: 10 -> 0, of which waited for: 6 -> 0; matrix products, arithmetic and copies ran while one was open for 10% -> 0% of each run, Pallas kernels for 0% -> 0%
where the time goes in v1:
time: 66.5 us; the launch traced here: 65.8 us
  Pallas kernels  49.8 us (75%)
  local copies, waits for them, and re-layouts  15.3 us (23%)
    pallas_call x1, Pallas kernels, local(): make_kernel(ny, ns, gx, scales)  49.8 us
    unnamed x28, local copies, waits for them, and re-layouts  13.9 us

profile of v1, /device:TPU:1, one launch (start us, length us, event | category | flops | bytes accessed | tf_op | source)
XLA Modules:
  0.0 65.8 jit_solution(18173741850202219170)
XLA Ops:
  0.6 0.8 %reshape.41.w1t = bf16[108,16]{1,0:T(8,128)(2,1)S(1)} reshape(bf16[3,3,3,4,16]{4,3,2,1,0:T(4,128)(2,1)} %bitcast.27) | data formatting | bytes 6912 | tf_op jit(solution)/shard_map/reshape | solution.py:487
  1.4 0.0 copy-start
  1.4 1.0 %copy-done = bf16[4,4,8,8,256]{4,3,2,1,0:T(8,128)(2,1)S(1)} copy-done((bf16[4,4,8,8,256]{4,3,2,1,0:T(8,128)(2,1)S(1)}, bf16[4,4,8,8,256]{4,3,2,1,0:T(8,128)(2,1)}, u32[]{:S(2)}) %copy-start) | copy-done | bytes 524312
  2.4 0.0 copy-start.1
  2.4 0.9 %copy-done.1 = bf16[64,32,3,3,3]{0,1,4,3,2:T(8,128)(2,1)S(1)} copy-done((bf16[64,32,3,3,3]{0,1,4,3,2:T(8,128)(2,1)S(1)}, bf16[64,32,3,3,3]{0,1,4,3,2:T(8,128)(2,1)}, u32[]{:S(2)}) %copy-start.1) | copy-done | bytes 110616
  3.4 0.0 copy-start.2
  3.4 0.9 %copy-done.2 = bf16[32,16,3,3,3]{0,1,4,3,2:T(8,128)(2,1)S(1)} copy-done((bf16[32,16,3,3,3]{0,1,4,3,2:T(8,128)(2,1)S(1)}, bf16[32,16,3,3,3]{0,1,4,3,2:T(8,128)(2,1)}, u32[]{:S(2)}) %copy-start.2) | copy-done | bytes 27672
  4.3 0.0 copy-start.3
  4.3 0.7 %copy-done.3 = bf16[1,64,1,128]{3,1,2,0:T(8,128)(2,1)S(1)} copy-done((bf16[1,64,1,128]{3,1,2,0:T(8,128)(2,1)S(1)}, bf16[1,64,1,128]{3,1,2,0:T(8,128)(2,1)}, u32[]{:S(2)}) %copy-start.3) | copy-done | bytes 16408
  5.0 0.0 copy-start.4
  5.0 1.4 %copy-done.4 = bf16[1024,768]{1,0:T(8,128)(2,1)S(1)} copy-done((bf16[1024,768]{1,0:T(8,128)(2,1)S(1)}, bf16[1024,768]{1,0:T(8,128)(2,1)}, u32[]{:S(2)}) %copy-start.4) | copy-done | bytes 1572888
  6.4 0.0 copy-start.5
  6.4 0.9 %copy-done.5 = bf16[256,384]{1,0:T(8,128)(2,1)S(1)} copy-done((bf16[256,384]{1,0:T(8,128)(2,1)S(1)}, bf16[256,384]{1,0:T(8,128)(2,1)}, u32[]{:S(2)}) %copy-start.5) | copy-done | bytes 196632
  7.3 0.0 copy-start.6
  7.3 0.9 %copy-done.6 = bf16[256,384]{1,0:T(8,128)(2,1)S(1)} copy-done((bf16[256,384]{1,0:T(8,128)(2,1)S(1)}, bf16[256,384]{1,0:T(8,128)(2,1)}, u32[]{:S(2)}) %copy-start.6) | copy-done | bytes 196632
  8.3 0.0 copy-start.7
  8.3 0.9 %copy-done.7 = bf16[256,384]{1,0:T(8,128)(2,1)S(1)} copy-done((bf16[256,384]{1,0:T(8,128)(2,1)S(1)}, bf16[256,384]{1,0:T(8,128)(2,1)}, u32[]{:S(2)}) %copy-start.7) | copy-done | bytes 196632
  9.2 0.0 copy-start.8
  9.2 0.9 %copy-done.8 = bf16[272,240]{1,0:T(8,128)(2,1)S(1)} copy-done((bf16[272,240]{1,0:T(8,128)(2,1)S(1)}, bf16[272,240]{1,0:T(8,128)(2,1)}, u32[]{:S(2)}) %copy-start.8) | copy-done | bytes 130584
  10.1 0.0 copy-start.9
  10.1 0.9 %copy-done.9 = bf16[256,256]{1,0:T(8,128)(2,1)S(1)} copy-done((bf16[256,256]{1,0:T(8,128)(2,1)S(1)}, bf16[256,256]{1,0:T(8,128)(2,1)}, u32[]{:S(2)}) %copy-start.9) | copy-done | bytes 131096
  11.0 0.0 copy-start.10
  11.0 0.8 %copy-done.10 = bf16[80,256]{1,0:T(8,128)(2,1)S(1)} copy-done((bf16[80,256]{1,0:T(8,128)(2,1)S(1)}, bf16[80,256]{1,0:T(8,128)(2,1)}, u32[]{:S(2)}) %copy-start.10) | copy-done | bytes 40984
  11.8 0.0 copy-start.11
  11.8 0.8 %copy-done.11 = bf16[144,108]{1,0:T(8,128)(2,1)S(1)} copy-done((bf16[144,108]{1,0:T(8,128)(2,1)S(1)}, bf16[144,108]{1,0:T(8,128)(2,1)}, u32[]{:S(2)}) %copy-start.11) | copy-done | bytes 31128
  12.5 49.8 %layers.1 = (bf16[64,128]{1,0:T(8,128)(2,1)S(1)}, bf16[4,256,128]{2,1,0:T(8,128)(2,1)S(1)}, f32[108,16]{1,0:T(8,128)S(1)}, f32[432,32]{1,0:T(8,128)S(1)}, f32[864,64]{1,0:T(8,128)S(1)}) custom-call(bf16[4,256,256]{2,1,0:T(8,128)(2,1)S(1)} %bitcast.22, bf16[108,16]{1,0:T(8,128)(2,1)S(1)} %reshape.41.w1t, bf16[432,32]{1,0:T(8,128)(2,1)S(1)} %bitcast.24, ...), custom_call_target="tpu_custom_call" | custom-call | flops 6000000000 | bytes 8000000 | tf_op jit(solution)/shard_map/layers/pallas_call | solution.py:490
  62.4 0.6 reshape.47
  63.0 0.6 copy.22
  63.7 0.7 %copy.23 = bf16[4,16,4,4,128]{4,3,2,1,0:T(4,128)(2,1)} copy(bf16[4,16,4,4,128]{4,3,2,1,0:T(4,128)(2,1)S(1)} %bitcast.19) | data formatting | bytes 524288
  64.4 0.7 %copy.24 = f32[32,16,3,3,3]{0,1,4,3,2:T(8,128)} copy(f32[32,16,3,3,3]{0,1,4,3,2:T(8,128)S(1)} %bitcast.20) | data formatting | bytes 110592
  65.0 0.8 %copy.25 = f32[64,32,3,3,3]{0,1,4,3,2:T(8,128)} copy(f32[64,32,3,3,3]{0,1,4,3,2:T(8,128)S(1)} %bitcast.18) | data formatting | bytes 442368
Async XLA Ops:
  1.4 1.0 %copy-start = (bf16[4,4,8,8,256]{4,3,2,1,0:T(8,128)(2,1)S(1)}, bf16[4,4,8,8,256]{4,3,2,1,0:T(8,128)(2,1)}, u32[]{:S(2)}) copy-start(bf16[4,4,8,8,256]{4,3,2,1,0:T(8,128)(2,1)} %param.13) | copy-start | bytes 1572868
  2.4 0.9 %copy-start.1 = (bf16[64,32,3,3,3]{0,1,4,3,2:T(8,128)(2,1)S(1)}, bf16[64,32,3,3,3]{0,1,4,3,2:T(8,128)(2,1)}, u32[]{:S(2)}) copy-start(bf16[64,32,3,3,3]{0,1,4,3,2:T(8,128)(2,1)} %param.16) | copy-start | bytes 331780
  3.4 0.9 %copy-start.2 = (bf16[32,16,3,3,3]{0,1,4,3,2:T(8,128)(2,1)S(1)}, bf16[32,16,3,3,3]{0,1,4,3,2:T(8,128)(2,1)}, u32[]{:S(2)}) copy-start(bf16[32,16,3,3,3]{0,1,4,3,2:T(8,128)(2,1)} %param.15) | copy-start | bytes 82948
  4.3 0.7 %copy-start.3 = (bf16[1,64,1,128]{3,1,2,0:T(8,128)(2,1)S(1)}, bf16[1,64,1,128]{3,1,2,0:T(8,128)(2,1)}, u32[]{:S(2)}) copy-start(bf16[1,64,1,128]{3,1,2,0:T(8,128)(2,1)} %param.17) | copy-start | bytes 49156
  5.0 1.4 %copy-start.4 = (bf16[1024,768]{1,0:T(8,128)(2,1)S(1)}, bf16[1024,768]{1,0:T(8,128)(2,1)}, u32[]{:S(2)}) copy-start(bf16[1024,768]{1,0:T(8,128)(2,1)} %constant.19.clone.pm) | copy-start | bytes 4718596
  6.4 0.9 %copy-start.5 = (bf16[256,384]{1,0:T(8,128)(2,1)S(1)}, bf16[256,384]{1,0:T(8,128)(2,1)}, u32[]{:S(2)}) copy-start(bf16[256,384]{1,0:T(8,128)(2,1)} %constant.18.clone.s3) | copy-start | bytes 589828
  7.3 0.9 %copy-start.6 = (bf16[256,384]{1,0:T(8,128)(2,1)S(1)}, bf16[256,384]{1,0:T(8,128)(2,1)}, u32[]{:S(2)}) copy-start(bf16[256,384]{1,0:T(8,128)(2,1)} %constant.17.clone.s2) | copy-start | bytes 589828
  8.3 0.9 %copy-start.7 = (bf16[256,384]{1,0:T(8,128)(2,1)S(1)}, bf16[256,384]{1,0:T(8,128)(2,1)}, u32[]{:S(2)}) copy-start(bf16[256,384]{1,0:T(8,128)(2,1)} %constant.16.clone.s1) | copy-start | bytes 589828
  9.2 0.9 %copy-start.8 = (bf16[272,240]{1,0:T(8,128)(2,1)S(1)}, bf16[272,240]{1,0:T(8,128)(2,1)}, u32[]{:S(2)}) copy-start(bf16[272,240]{1,0:T(8,128)(2,1)} %constant.20.clone.ph) | copy-start | bytes 391684
  10.1 0.9 %copy-start.9 = (bf16[256,256]{1,0:T(8,128)(2,1)S(1)}, bf16[256,256]{1,0:T(8,128)(2,1)}, u32[]{:S(2)}) copy-start(bf16[256,256]{1,0:T(8,128)(2,1)} %constant.23.clone.po) | copy-start | bytes 393220
  11.0 0.8 %copy-start.10 = (bf16[80,256]{1,0:T(8,128)(2,1)S(1)}, bf16[80,256]{1,0:T(8,128)(2,1)}, u32[]{:S(2)}) copy-start(bf16[80,256]{1,0:T(8,128)(2,1)} %constant.21.clone.pq) | copy-start | bytes 122884
  11.8 0.8 %copy-start.11 = (bf16[144,108]{1,0:T(8,128)(2,1)S(1)}, bf16[144,108]{1,0:T(8,128)(2,1)}, u32[]{:S(2)}) copy-start(bf16[144,108]{1,0:T(8,128)(2,1)} %constant.22.clone.pw) | copy-start | bytes 93316

commit v2 on v0

v2 whole, which is shorter than its diff:
```python
import math

import jax
import jax.numpy as jnp
from jax import lax
from jax.experimental import pallas as pl
from jax.experimental.pallas import tpu as pltpu
from jax.sharding import PartitionSpec as P

GRAD_GAIN = 4.0
MESH = pl.DeviceIdType.MESH
F32 = jnp.float32
BF16 = jnp.bfloat16
TAPS_THREE = {-1: (1, 2), 0: (0, 1)}
TAPS_TWO = {-1: (2,), 0: (0, 1, 2), 1: (0, 1)}
COPIES = 192


def mm(a, b):
    return jnp.dot(a, b, preferred_element_type=F32)


def mm_t(a, b):
    return lax.dot_general(a, b, (((1,), (1,)), ((), ())), preferred_element_type=F32)


def activate(p):
    square = p * p + 1.0
    inverse = lax.rsqrt(square)
    active = (0.65 * p + 0.35 * (square * inverse - 1.0)).astype(BF16)
    slope = (0.65 + 0.35 * (p * inverse)).astype(BF16)
    return active, slope


def identity(n):
    return (
        lax.broadcasted_iota(jnp.int32, (n, n), 0) == lax.broadcasted_iota(jnp.int32, (n, n), 1)
    ).astype(F32).astype(BF16)


def grid(rows, lanes):
    return (
        lax.broadcasted_iota(jnp.int32, (rows, lanes), 0),
        lax.broadcasted_iota(jnp.int32, (rows, lanes), 1),
    )


def marks(condition):
    return condition.astype(F32).astype(BF16)


def make_kernel(ny, ns, nx, scales):
    n_near, n_far = ny * nx, ns // nx
    rows3, rows2 = 512 // n_near, 128 // n_near

    def kernel(vol_in, w1t_in, w2t_in, w3t_in, fg_in, feat_out, gact_out, o1_out, o2_out, o3_out,
               vol, w1t, w2t, w3t, fg, ls, feat, gact, o1, o2, o3, os,
               s1, s2, s3, pm, w1, w2, w3, w2k, w3k, hs, hr, vsm, e1, a1, sl1, e2, a2, sl2, e3, fgs, fts,
               g3, gg3, g2e, gg2, d1b, wb3, r3, z3, f3, wb2, r2, z2, f2, y1, z1, ss, rs):
        y = lax.axis_index("sample")
        s = lax.axis_index("space")
        z_me = lax.div(s, 2 * nx)
        x_me = lax.div(lax.rem(s, 2 * nx), 2)
        core = lax.rem(s, 2)
        near_me = y * nx + x_me
        far_me = z_me * 2 + core
        near_ids = [lax.rem(near_me + d, n_near) for d in range(1, n_near)]
        far_ids = [lax.rem(far_me + d, n_far) for d in range(1, n_far)]
        near = [
            {"sample": lax.div(m, nx), "space": z_me * 2 * nx + lax.rem(m, nx) * 2 + core} for m in near_ids
        ]
        far = [
            {"sample": y, "space": lax.div(m, 2) * 2 * nx + x_me * 2 + lax.rem(m, 2)} for m in far_ids
        ]
        y_peers = [{"sample": lax.rem(y + d, ny), "space": s} for d in range(1, ny)]
        y_prev, y_next = lax.rem(y + ny - 1, ny), lax.rem(y + 1, ny)
        s_prev, s_next = lax.rem(s + ns - 1, ns), lax.rem(s + 1, ns)
        prev = [
            {"sample": y, "space": s_prev},
            {"sample": y_prev, "space": s},
            {"sample": y_prev, "space": s_prev},
        ]
        following = [
            {"sample": y, "space": s_next},
            {"sample": y_next, "space": s},
            {"sample": y_next, "space": s_next},
        ]
        started = []
        stores = []

        def send(src, dst, device):
            n = len(started)
            copy = pltpu.make_async_remote_copy(
                src_ref=src, dst_ref=dst, send_sem=ss.at[n], recv_sem=rs.at[n],
                device_id=device, device_id_type=MESH,
            )
            copy.start()
            started.append(copy)
            return copy

        def arrive(*copies):
            for copy in copies:
                copy.wait_recv()

        def store(src, dst):
            copy = pltpu.make_async_copy(src, dst, os.at[len(stores)])
            copy.start()
            stores.append(copy)

        barrier = pltpu.get_barrier_semaphore()
        greeted = [prev[0], following[0], prev[2], following[2]] + near + far
        for device in greeted:
            pl.semaphore_signal(barrier, inc=1, device_id=device, device_id_type=MESH)

        loads = {}
        for n, (name, src, dst) in enumerate((
            ("vol", vol_in, vol), ("fg", fg_in, fg), ("w1t", w1t_in, w1t), ("w2t", w2t_in, w2t), ("w3t", w3t_in, w3t),
        )):
            loads[name] = pltpu.make_async_copy(src, dst, ls.at[n])
            loads[name].start()

        def loaded(*names):
            for name in names:
                loads.pop(name).wait()

        more_x = jnp.where(s == ns - 1, 0.0, 1.0).astype(F32)
        more_y = jnp.where(y == ny - 1, 0.0, 1.0).astype(F32)
        less_x = jnp.where(s == 0, 0.0, 1.0).astype(F32)
        less_y = jnp.where(y == 0, 0.0, 1.0).astype(F32)
        more_xy = more_x * more_y

        row, lane = grid(80, 256)
        edge = marks(
            ((row < 32) & (lane == (row >> 3) * 64 + (row & 7)))
            | ((row >= 32) & (row < 64) & (lane == (row - 32) * 8))
            | ((row >= 64) & (row < 68) & (lane == (row - 64) * 64))
        )
        for ref, last in ((s1, 127), (s2, 63), (s3, 31)):
            row, lane = grid(256, 128)
            for f in range(3):
                hit = row == 2 * lane + f
                if f == 2:
                    hit = hit & ((lane & last) != last)
                ref[:, f * 128:(f + 1) * 128] = marks(hit)
        row, lane = grid(128, 96)
        pm[...] = marks(((row & 15) == (lane >> 3)) & ((row >> 4) == (lane & 7)))

        loaded("vol", "fg")
        for b in range(4):
            hs[b] = mm(edge, vol[b]).astype(BF16)
        fgs[y] = fg[...]
        pl.semaphore_wait(barrier, len(greeted))
        vol_row = send(hs.at[:, pl.ds(32, 32)], hr.at[:, pl.ds(32, 32)], prev[1])
        vol_plane = send(hs.at[:, pl.ds(0, 32)], hr.at[:, pl.ds(0, 32)], prev[0])
        vol_corner = send(hs.at[:, pl.ds(64, 16)], hr.at[:, pl.ds(64, 16)], prev[2])

        for b in range(4):
            part = mm(vol[b], s1[...]).reshape(4, 8, 8, 384)
            for x in range(8):
                rows = part[:, x].reshape(32, 384)
                rows = jnp.concatenate([rows[:, f * 128:(f + 1) * 128] for f in range(3)], axis=0)
                vsm[x, :, b * 128:(b + 1) * 128] = rows.astype(BF16)
        for x in range(8):
            e1[x, 0:8] = mm(pm[...], vsm[x]).astype(BF16).reshape(8, 16, 512)
        loaded("w1t", "w2t", "w3t")
        row, lane = grid(144, 108)
        pads = marks((lane == (row >> 4) * 12 + (row & 15)) & ((row & 15) < 12))
        w1rows = w1t[...].astype(F32).reshape(108, 16).astype(BF16)
        w1[...] = mm_t(identity(16), mm(pads, w1rows).astype(BF16)).astype(BF16)
        w2[...] = mm_t(identity(32), w2t[...]).astype(BF16)

        def columns_one(i, j):
            return jnp.concatenate(
                [e1[2 * i + a, 2 * j:2 * j + 3].reshape(48, 512) for a in range(3)], axis=0
            )

        def cell_one(i, j):
            act, slope = activate(mm(w1[...], columns_one(i, j)))
            a1[i, j] = act
            sl1[i * 4 + j] = slope

        def widen_two(cells, keep=None):
            rows = jnp.concatenate([a1[i, j] for i, j in cells], axis=0)
            rows = jnp.concatenate([rows[:, :256], rows[:, 256:]], axis=0)
            part = mm(rows, s2[...])
            if keep is not None:
                part = part * keep
            part = part.astype(BF16).reshape(2, len(cells), 16, 384)
            for p in range(2):
                for n, (i, j) in enumerate(cells):
                    for f in range(3):
                        e2[i, j, f * 16:(f + 1) * 16, p * 128:(p + 1) * 128] = (
                            part[p, n, :, f * 128:(f + 1) * 128]
                        )

        def columns_two(i, j):
            return jnp.concatenate(
                [e2[2 * i + a, 2 * j:2 * j + 3].reshape(144, 256) for a in range(3)], axis=0
            )

        def cell_two(i, j):
            act, slope = activate(mm(w2[...], columns_two(i, j)))
            a2[i, j] = act
            sl2[i + 1, j + 1] = slope

        def widen_three(cells, keep=None):
            part = mm(jnp.concatenate([a2[i, j] for i, j in cells], axis=0), s3[...])
            if keep is not None:
                part = part * keep
            part = part.astype(BF16).reshape(len(cells), 32, 384)
            for n, (i, j) in enumerate(cells):
                for f in range(3):
                    e3[i, j, f * 32:(f + 1) * 32, :] = part[n, :, f * 128:(f + 1) * 128]

        for i in range(3):
            cell_one(i, 0)
        act_row = send(a1.at[pl.ds(0, 3), 0], a1.at[pl.ds(0, 3), 4], prev[1])
        for j in range(1, 3):
            cell_one(0, j)
        act_plane = send(a1.at[0, pl.ds(0, 3)], a1.at[4, pl.ds(0, 3)], prev[0])
        act_corner = send(a1.at[0, 0], a1.at[4, 4], prev[2])
        for i in range(1, 3):
            for j in range(1, 3):
                cell_one(i, j)
        widen_two([(i, j) for i in range(3) for j in range(3)])
        cell_two(0, 0)
        two_row = send(a2.at[0, 0], a2.at[0, 2], prev[1])
        two_plane = send(a2.at[0, 0], a2.at[2, 0], prev[0])
        two_corner = send(a2.at[0, 0], a2.at[2, 2], prev[2])
        got_fg = [send(fgs.at[y], fgs.at[y], device) for device in y_peers]
        widen_three([(0, 0)])

        w3[...] = mm_t(identity(64), w3t[...]).astype(BF16)
        w2rows = w2t[...].reshape(9, 3, 16, 32)
        w3rows = w3t[...].reshape(9, 3, 32, 64)
        for f in range(3):
            w2k[:, f * 32:(f + 1) * 32] = w2rows[:, f].reshape(144, 32)
            w3k[:, f * 64:(f + 1) * 64] = w3rows[:, f].reshape(288, 64)
        row, lane = grid(512, 128)
        regroup = marks(row == (lane >> 5) * 128 + y * 32 + (lane & 31))

        def widen_volume(at, keep):
            part = mm(hr[:, at:at + 32].reshape(128, 256), s1[...]) * keep
            rows = jnp.concatenate(
                [
                    jnp.concatenate(
                        [part[b * 32:(b + 1) * 32, f * 128:(f + 1) * 128] for f in range(3)], axis=0
                    )
                    for b in range(4)
                ],
                axis=1,
            )
            return mm(pm[...], rows.astype(BF16)).astype(BF16).reshape(8, 16, 512)

        arrive(vol_plane)
        e1[8, 0:8] = widen_volume(0, more_x)
        cell_one(3, 0)
        act_row_end = send(a1.at[3, 0], a1.at[3, 4], prev[1])
        arrive(vol_row)
        block = widen_volume(32, more_y)
        for x in range(8):
            e1[x, 8] = block[x]
        cell_one(0, 3)
        act_plane_end = send(a1.at[0, 3], a1.at[4, 3], prev[0])
        for n in range(1, 3):
            cell_one(n, 3)
            cell_one(3, n)
        widen_two([(3, 0), (3, 1), (3, 2)])
        arrive(act_plane)
        widen_two([(4, 0), (4, 1), (4, 2)], more_x)
        cell_two(1, 0)
        two_row_end = send(a2.at[1, 0], a2.at[1, 2], prev[1])
        widen_two([(0, 3), (1, 3), (2, 3)])
        arrive(act_row)
        widen_two([(0, 4), (1, 4), (2, 4)], more_y)
        cell_two(0, 1)
        two_plane_end = send(a2.at[0, 1], a2.at[2, 1], prev[0])
        widen_three([(0, 1), (1, 0)])
        arrive(*got_fg)
        cotangent = mm(jnp.concatenate([fgs[k] for k in range(4)], axis=1), regroup)
        arrive(vol_corner)
        part = mm(hr[:, 64:80].reshape(64, 256), s1[...]) * more_xy
        rows = jnp.concatenate(
            [
                jnp.concatenate(
                    [part[b * 16:(b + 1) * 16, f * 128:(f + 1) * 128] for f in range(3)], axis=0
                )
                for b in range(4)
            ],
            axis=1,
        )
        row, lane = grid(16, 48)
        picked = marks((row == (lane >> 4) * 4 + (lane & 15)) & ((lane & 15) < 4))
        e1[8, 8] = mm(picked, rows.astype(BF16)).astype(BF16)
        cell_one(3, 3)
        widen_two([(3, 3)])
        arrive(act_corner)
        widen_two([(4, 4)], more_xy)
        arrive(act_plane_end)
        widen_two([(4, 3)], more_x)
        arrive(act_row_end)
        widen_two([(3, 4)], more_y)
        cell_two(1, 1)
        got_slope = [
            send(sl2.at[2, pl.ds(1, 2)], sl2.at[0, pl.ds(1, 2)], following[0]),
            send(sl2.at[pl.ds(1, 2), 2], sl2.at[pl.ds(1, 2), 0], following[1]),
            send(sl2.at[2, 2], sl2.at[0, 0], following[2]),
        ]
        widen_three([(1, 1)])
        arrive(two_row, two_row_end)
        widen_three([(0, 2), (1, 2)], more_y)
        arrive(two_plane, two_plane_end)
        widen_three([(2, 0), (2, 1)], more_x)
        arrive(two_corner)
        widen_three([(2, 2)], more_xy)

        columns_three = e3[...].reshape(864, 128)
        act, slope = activate(mm(w3[...], columns_three))
        grad_three = (cotangent * slope.astype(F32)).astype(BF16)
        g3[3] = grad_three
        got_grad = [send(g3.at[3], g3.at[to], following[i]) for i, to in ((2, 0), (1, 2), (0, 1))]

        part = mm_t(columns_three, grad_three)
        part = jnp.concatenate([part[:432], part[432:]], axis=1)
        wb3[...] = jnp.zeros_like(wb3)
        for n in range(27):
            group, at = divmod(n * 16, rows3)
            wb3[group, at:at + 16] = part[n * 16:(n + 1) * 16]
        got_r3 = [send(wb3.at[m], r3.at[d], near[d]) for d, m in enumerate(near_ids)]
        fts[y] = act
        got_feat = [send(fts.at[y], fts.at[y], device) for device in y_peers]

        arrive(*got_grad)
        row, lane = grid(256, 128)
        inside = jnp.where(
            row < 64, less_x * less_y, jnp.where(row < 128, less_x, jnp.where(row < 192, less_y, 1.0))
        )
        rows = (g3[...].reshape(256, 128).astype(F32) * inside).astype(BF16)
        for f in range(3):
            part = mm_t(rows, s3[:, f * 128:(f + 1) * 128]).astype(BF16)
            gg3[:, f * 64:(f + 1) * 64, :] = part.reshape(4, 64, 256)

        def spread(taps, weights, widened, width, channels):
            down = {}
            for i in taps:
                for j in taps:
                    pairs = [(a, e) for a in taps[i] for e in taps[j]]
                    picked = jnp.concatenate(
                        [weights[(a * 3 + e) * channels:(a * 3 + e + 1) * channels, :] for a, e in pairs], axis=0
                    )
                    part = mm(picked, widened[(i + 1) * width + j + 1])
                    for n, (a, e) in enumerate(pairs):
                        key = (2 * i + a, 2 * j + e)
                        term = part[n * channels:(n + 1) * channels]
                        down[key] = term if key not in down else down[key] + term
            return down

        down = spread(TAPS_THREE, w3k, gg3, 2, 32)
        arrive(*got_slope)
        for i in range(-1, 2):
            for j in range(-1, 2):
                rounded = down[i, j].astype(BF16).astype(F32)
                g2e[(i + 1) * 3 + j + 1] = (rounded * sl2[i + 1, j + 1].astype(F32)).astype(BF16)

        part = None
        for i in range(2):
            for j in range(2):
                term = mm_t(columns_two(i, j), g2e[(i + 1) * 3 + j + 1])
                part = term if part is None else part + term
        wb2[...] = jnp.zeros_like(wb2)
        for n in range(54):
            lanes, at = divmod(n * 8, 112)
            group, at = divmod(at, rows2)
            wb2[group, at:at + 8, lanes * 32:(lanes + 1) * 32] = part[n * 8:(n + 1) * 8]
        got_r2 = [send(wb2.at[m], r2.at[d], near[d]) for d, m in enumerate(near_ids)]

        for p in range(2):
            rows = g2e[...].reshape(288, 256)[:, p * 128:(p + 1) * 128]
            for f in range(3):
                part = mm_t(rows, s2[:, f * 128:(f + 1) * 128]).astype(BF16)
                gg2[:, f * 32:(f + 1) * 32, p * 256:(p + 1) * 256] = part.reshape(9, 32, 256)
        down = spread(TAPS_TWO, w2k, gg2, 3, 16)

        part = None
        for i in range(4):
            for j in range(4):
                d1b[(i * 4 + j) * 16:(i * 4 + j + 1) * 16, :] = down[i, j].astype(BF16)
                grad_one = (down[i, j] * sl1[i * 4 + j].astype(F32)).astype(BF16)
                term = mm_t(columns_one(i, j), grad_one)
                part = term if part is None else part + term
        part = jnp.concatenate([part[t * 16:t * 16 + 12] for t in range(9)] + [jnp.zeros((20, 16), F32)], axis=0)
        y1[near_me] = part.T
        got_y1 = [send(y1.at[near_me], y1.at[near_me], device) for device in near]

        def total(first, refs):
            value = first
            for ref in refs:
                value = value + ref
            return value

        arrive(*got_r3)
        z3[far_me] = total(wb3[near_me], [r3[d] for d in range(n_near - 1)])
        got_z3 = [send(z3.at[far_me], z3.at[far_me], device) for device in far]
        row, lane = grid(256, 256)
        swap = marks(((row >> 4) == (lane & 15)) & ((row & 15) == (lane >> 4)))
        block = mm(swap, d1b[...]).astype(BF16)
        for b in range(4):
            gact[b] = block[:, b * 128:(b + 1) * 128]
        store(gact, gact_out)
        arrive(*got_feat)
        feat[...] = mm(jnp.concatenate([fts[k] for k in range(4)], axis=1), regroup).astype(BF16)
        store(feat, feat_out)
        arrive(*got_r2)
        z2[far_me] = total(wb2[near_me], [r2[d] for d in range(n_near - 1)])
        got_z2 = [send(z2.at[far_me], z2.at[far_me], device) for device in far]
        arrive(*got_y1)
        z1[far_me] = total(y1[0], [y1[m] for m in range(1, n_near)])
        got_z1 = [send(z1.at[far_me], z1.at[far_me], device) for device in far]

        arrive(*got_z3)
        f3[near_me] = total(z3[0], [z3[m] for m in range(1, n_far)]) * scales[2]
        got_f3 = [send(f3.at[near_me], f3.at[near_me], device) for device in near]
        arrive(*got_z2)
        f2[near_me] = total(z2[0], [z2[m] for m in range(1, n_far)]) * scales[1]
        got_f2 = [send(f2.at[near_me], f2.at[near_me], device) for device in near]
        arrive(*got_z1)
        part = total(z1[0], [z1[m] for m in range(1, n_far)]) * scales[0]
        o1[...] = part.T[:108].reshape(27, 4, 16)
        store(o1, o1_out)
        arrive(*got_f3)
        part = f3[...].reshape(512, 128)[:432]
        for half in range(2):
            o3[half * 432:(half + 1) * 432, :] = part[:, half * 64:(half + 1) * 64]
        store(o3, o3_out)
        arrive(*got_f2)
        part = f2[...].reshape(128, 128)
        for n in range(27):
            lanes, at = divmod(n * 16, 112)
            o2[n * 16:(n + 1) * 16, :] = part[at:at + 16, lanes * 32:(lanes + 1) * 32]
        store(o2, o2_out)
        for copy in started:
            copy.wait_send()
        for copy in stores:
            copy.wait()

    vm = pltpu.VMEM
    scratch = [
        vm((4, 256, 256), BF16), vm((27, 4, 16), BF16), vm((432, 32), BF16), vm((864, 64), BF16), vm((64, 128), BF16),
        pltpu.SemaphoreType.DMA((5,)),
        vm((64, 128), BF16), vm((4, 256, 128), BF16), vm((27, 4, 16), F32), vm((432, 32), F32), vm((864, 64), F32),
        pltpu.SemaphoreType.DMA((5,)),
        vm((256, 384), BF16), vm((256, 384), BF16), vm((256, 384), BF16), vm((128, 96), BF16),
        vm((16, 144), BF16), vm((32, 432), BF16), vm((64, 864), BF16), vm((144, 96), BF16), vm((288, 192), BF16),
        vm((4, 80, 256), BF16), vm((4, 80, 256), BF16), vm((8, 96, 512), BF16),
        vm((9, 9, 16, 512), BF16), vm((5, 5, 16, 512), BF16), vm((16, 16, 512), BF16), vm((5, 5, 48, 256), BF16),
        vm((3, 3, 32, 256), BF16), vm((3, 3, 32, 256), BF16), vm((3, 3, 96, 128), BF16),
        vm((4, 64, 128), BF16), vm((4, 64, 128), BF16), vm((4, 64, 128), BF16), vm((4, 192, 256), BF16),
        vm((9, 32, 256), BF16), vm((9, 96, 512), BF16), vm((256, 512), BF16),
        vm((n_near, rows3, 128), F32), vm((n_near - 1, rows3, 128), F32), vm((n_far, rows3, 128), F32),
        vm((n_near, rows3, 128), F32),
        vm((n_near, rows2, 128), F32), vm((n_near - 1, rows2, 128), F32), vm((n_far, rows2, 128), F32),
        vm((n_near, rows2, 128), F32),
        vm((n_near, 16, 128), F32), vm((n_far, 16, 128), F32),
        pltpu.SemaphoreType.DMA((COPIES,)), pltpu.SemaphoreType.DMA((COPIES,)),
    ]
    return pl.pallas_call(
        kernel,
        out_shape=(
            jax.ShapeDtypeStruct((64, 128), BF16),
            jax.ShapeDtypeStruct((4, 256, 128), BF16),
            jax.ShapeDtypeStruct((27, 4, 16), F32),
            jax.ShapeDtypeStruct((432, 32), F32),
            jax.ShapeDtypeStruct((864, 64), F32),
        ),
        in_specs=[pl.BlockSpec(memory_space=pltpu.HBM)] * 5,
        out_specs=[pl.BlockSpec(memory_space=pltpu.HBM)] * 5,
        scratch_shapes=scratch,
        compiler_params=pltpu.CompilerParams(
            collective_id=0, has_side_effects=True, vmem_limit_bytes=60 * 1024 * 1024
        ),
        cost_estimate=pl.CostEstimate(flops=3_000_000_000, bytes_accessed=4_000_000, transcendentals=0),
        name="layers",
    )


def hand_over(*refs):
    given, results, held, (sems,) = refs[:5], refs[5:10], refs[10:15], refs[15:]
    come = [pltpu.make_async_copy(given[n], held[n], sems.at[n]) for n in range(5)]
    go = [pltpu.make_async_copy(held[n], results[n], sems.at[5 + n]) for n in range(5)]
    for copy in come:
        copy.start()
    for n in (0, 2, 3, 4, 1):
        come[n].wait()
        go[n].start()
    for copy in go:
        copy.wait()


def solution(mesh):
    ny, ns = mesh.shape["sample"], mesh.shape["space"]
    nx = 4 if ns % 8 == 0 else 2

    def local(volumes, weight_one, weight_two, weight_three, feature_grad):
        cells = volumes.shape[0] * volumes.shape[2] * ns * volumes.shape[3] * ny * volumes.shape[4]
        scales = [GRAD_GAIN / math.sqrt(cells // 8**n) for n in (1, 2, 3)]
        flat = [
            jnp.transpose(w, (2, 3, 4, 1, 0)).reshape(shape)
            for w, shape in ((weight_one, (27, 4, 16)), (weight_two, (432, 32)), (weight_three, (864, 64)))
        ]
        features, grad_act, one, two, three = make_kernel(ny, ns, nx, scales)(
            volumes.reshape(4, 256, 256), *flat, feature_grad.reshape(64, 128)
        )

        features, grad_act, one, two, three = pl.pallas_call(
            hand_over,
            out_shape=(
                jax.ShapeDtypeStruct((64, 128), BF16),
                jax.ShapeDtypeStruct((4, 256, 128), BF16),
                jax.ShapeDtypeStruct((27, 4, 16), F32),
                jax.ShapeDtypeStruct((432, 32), F32),
                jax.ShapeDtypeStruct((864, 64), F32),
            ),
            in_specs=[pl.BlockSpec(memory_space=pltpu.HBM)] * 5,
            out_specs=[pl.BlockSpec(memory_space=pltpu.HBM)] * 5,
            scratch_shapes=[
                pltpu.VMEM((64, 128), BF16), pltpu.VMEM((4, 256, 128), BF16), pltpu.VMEM((27, 4, 16), F32),
                pltpu.VMEM((432, 32), F32), pltpu.VMEM((864, 64), F32), pltpu.SemaphoreType.DMA((10,)),
            ],
            compiler_params=pltpu.CompilerParams(vmem_limit_bytes=63 * 1024 * 1024),
            name="hand_over",
        )(features, grad_act, one, two, three)

        def filters(array, channels):
            return jnp.transpose(array.reshape(3, 3, 3, channels, -1), (4, 3, 0, 1, 2))

        return (
            features.reshape(feature_grad.shape),
            grad_act.reshape(4, 16, 4, 4, 128),
            filters(one, 4),
            filters(two, 16),
            filters(three, 32),
        )

    in_specs = (
        P(None, None, "space", "sample", None),
        P(),
        P(),
        P(),
        P("sample", None, "space", None),
    )
    out_specs = (
        P("sample", None, "space", None),
        P(None, None, "space", "sample", None),
        P(),
        P(),
        P(),
    )
    return jax.shard_map(local, mesh=mesh, in_specs=in_specs, out_specs=out_specs, check_vma=False)
```

time: 571 us -> 53.8 us (0.09); the launches traced: 561 us -> 53.6 us
  waiting for transfers between devices: 222 us -> 0 us
  local copies, waits for them, and re-layouts: 129 us -> 0 us
  blocking collectives: 87.7 us -> 0 us
  Pallas kernels: 0 us -> 53 us
  matrix products: 49.9 us -> 0 us
  other arithmetic: 29.2 us -> 0 us
  starting transfers between devices: 28.3 us -> 0 us
  between operations: 15.3 us -> 0.64 us
    psum x1 -> x0, waiting for transfers between devices: 208 us -> none  [local(): lax.psum((filter_grad(input_one, grad_one, block_pads), filter_grad(input...]
    psum x1 -> x0, blocking collectives: 79.1 us -> none  [local(): lax.psum((filter_grad(input_one, grad_one, block_pads), filter_grad(input...]
    conv_general_dilated x20 -> x0, local copies, waits for them, and re-layouts: 62.3 us -> none  [the longest x8 54.6 us: strided_conv(): lax.conv_general_dilated(padded, weights, (2, 2, 2), paddings, dimension_...]
    pallas_call x0 -> x2, Pallas kernels: none -> 53 us  [the longest x1 50.8 us: local(): make_kernel(ny, ns, nx, scales)]
    conv_general_dilated x8 -> x0, matrix products: 49.9 us -> none  [the longest x3 34.5 us: filter_grad(): lax.conv_general_dilated(padded, gradient, (1, 1, 1), paddings, rhs_dilat...]
    concatenate x9 -> x0, local copies, waits for them, and re-layouts: 35.7 us -> none  [the longest x3 20.8 us: with_next_block(): return jnp.concatenate([widened, edge_row], axis=3)]
    ppermute x8 -> x0, starting transfers between devices: 24.8 us -> none  [shifted(): return lax.ppermute(block, axis, route)]
    concatenate x4 -> x0, other arithmetic: 18.6 us -> none  [the longest x2 17.1 us: with_next_block(): return jnp.concatenate([widened, edge_row], axis=3)]
  transfers between devices with their start and end apart: 10 -> 0, of which waited for: 6 -> 0; matrix products, arithmetic and copies ran while one was open for 10% -> 0% of each run, Pallas kernels for 0% -> 0%
where the time goes in v2:
time: 53.8 us; the launch traced here: 53.6 us
  Pallas kernels  53 us (99%)
  between operations  0.64 us (1%)
    pallas_call x1, Pallas kernels, local(): make_kernel(ny, ns, nx, scales)  50.8 us
    pallas_call x1, Pallas kernels, local(): pl.pallas_call(hand_over, out_shape=(jax.ShapeDtypeStruct((64, 128), BF16...  2.18 us

profile of v2, /device:TPU:1, one launch (start us, length us, event | category | flops | bytes accessed | tf_op | source)
XLA Modules:
  0.0 53.6 jit_solution(7657642025114225924)
XLA Ops:
  0.6 50.8 %layers.1 = (bf16[64,128]{1,0:T(8,128)(2,1)}, bf16[4,256,128]{2,1,0:T(8,128)(2,1)}, f32[27,4,16]{2,1,0:T(4,128)}, f32[432,32]{1,0:T(8,128)}, f32[864,64]{1,0:T(8,128)}) custom-call(bf16[4,256,256]{2,1,0:T(8,128)(2,1)} %bitcast.22, bf16[27,4,16]{2,1,0:T(4,128)(2,1)} %bitcast.29, bf16[432,32]{1,0:T(8,128)(2,1)} %bitcast.27, bf16[864,64]{1,0:T(8,128)(2,1)} %bitcast.25, ...), custom_call_target="tpu_custom_call" | custom-call | flops 3000000000 | bytes 4000000 | tf_op jit(solution)/shard_map/layers/pallas_call | solution.py:510
  51.4 2.2 %hand_over.1 = (bf16[64,128]{1,0:T(8,128)(2,1)}, bf16[4,256,128]{2,1,0:T(8,128)(2,1)}, f32[27,4,16]{2,1,0:T(4,128)}, f32[432,32]{1,0:T(8,128)}, f32[864,64]{1,0:T(8,128)}) custom-call(bf16[64,128]{1,0:T(8,128)(2,1)} %get-tuple-element.15.refs_0_, bf16[4,256,128]{2,1,0:T(8,128)(2,1)} %get-tuple-element.16.refs_1_, f32[27,4,16]{2,1,0:T(4,128)} %get-tuple-element.17.refs_2_, ...), custom_call_target="tpu_custom_call" | custom-call | tf_op jit(solution)/shard_map/hand_over/pallas_call | solution.py:514

commit v3 on v2

--- a/solution.py
+++ b/solution.py
@@ -13,7 +13,7 @@
 BF16 = jnp.bfloat16
 TAPS_THREE = {-1: (1, 2), 0: (0, 1)}
 TAPS_TWO = {-1: (2,), 0: (0, 1, 2), 1: (0, 1)}
-COPIES = 192
+COPIES = 29
 
 
 def mm(a, b):
@@ -50,7 +50,7 @@
 
 
 def make_kernel(ny, ns, nx, scales):
-    n_near, n_far = ny * nx, ns // nx
+    n_near, n_far = ny * nx * 2, ns // (2 * nx)
     rows3, rows2 = 512 // n_near, 128 // n_near
 
     def kernel(vol_in, w1t_in, w2t_in, w3t_in, fg_in, feat_out, gact_out, o1_out, o2_out, o3_out,
@@ -62,16 +62,14 @@
         z_me = lax.div(s, 2 * nx)
         x_me = lax.div(lax.rem(s, 2 * nx), 2)
         core = lax.rem(s, 2)
-        near_me = y * nx + x_me
-        far_me = z_me * 2 + core
+        near_me = (y * nx + x_me) * 2 + core
+        far_me = z_me
         near_ids = [lax.rem(near_me + d, n_near) for d in range(1, n_near)]
         far_ids = [lax.rem(far_me + d, n_far) for d in range(1, n_far)]
         near = [
-            {"sample": lax.div(m, nx), "space": z_me * 2 * nx + lax.rem(m, nx) * 2 + core} for m in near_ids
+            {"sample": lax.div(m, 2 * nx), "space": z_me * 2 * nx + lax.rem(m, 2 * nx)} for m in near_ids
         ]
-        far = [
-            {"sample": y, "space": lax.div(m, 2) * 2 * nx + x_me * 2 + lax.rem(m, 2)} for m in far_ids
-        ]
+        far = [{"sample": y, "space": m * 2 * nx + x_me * 2 + core} for m in far_ids]
         y_peers = [{"sample": lax.rem(y + d, ny), "space": s} for d in range(1, ny)]
         y_prev, y_next = lax.rem(y + ny - 1, ny), lax.rem(y + 1, ny)
         s_prev, s_next = lax.rem(s + ns - 1, ns), lax.rem(s + 1, ns)
@@ -87,16 +85,34 @@
         ]
         started = []
         stores = []
-
-        def send(src, dst, device):
-            n = len(started)
+        used = []
+
+        def push(src, dst, device, n):
             copy = pltpu.make_async_remote_copy(
                 src_ref=src, dst_ref=dst, send_sem=ss.at[n], recv_sem=rs.at[n],
                 device_id=device, device_id_type=MESH,
             )
             copy.start()
-            started.append(copy)
             return copy
+
+        def send(src, dst, device):
+            used.append(None)
+            started.append(push(src, dst, device, len(used) - 1))
+            return started[-1]
+
+        def send_all(copies, landed):
+            used.append(None)
+            n = len(used) - 1
+            for src, dst, device in copies:
+                push(src, dst, device, n)
+            return landed, n
+
+        def arrive_all(group):
+            landed, n = group
+            pltpu.make_async_copy(landed, landed, rs.at[n]).wait()
+            grouped.append(group)
+
+        grouped = []
 
         def arrive(*copies):
             for copy in copies:
@@ -227,7 +243,7 @@
         two_row = send(a2.at[0, 0], a2.at[0, 2], prev[1])
         two_plane = send(a2.at[0, 0], a2.at[2, 0], prev[0])
         two_corner = send(a2.at[0, 0], a2.at[2, 2], prev[2])
-        got_fg = [send(fgs.at[y], fgs.at[y], device) for device in y_peers]
+        got_fg = send_all([(fgs.at[y], fgs.at[y], device) for device in y_peers], fgs.at[pl.ds(0, ny - 1)])
         widen_three([(0, 0)])
 
         w3[...] = mm_t(identity(64), w3t[...]).astype(BF16)
@@ -276,7 +292,7 @@
         cell_two(0, 1)
         two_plane_end = send(a2.at[0, 1], a2.at[2, 1], prev[0])
         widen_three([(0, 1), (1, 0)])
-        arrive(*got_fg)
+        arrive_all(got_fg)
         cotangent = mm(jnp.concatenate([fgs[k] for k in range(4)], axis=1), regroup)
         arrive(vol_corner)
         part = mm(hr[:, 64:80].reshape(64, 256), s1[...]) * more_xy
@@ -326,9 +342,9 @@
         for n in range(27):
             group, at = divmod(n * 16, rows3)
             wb3[group, at:at + 16] = part[n * 16:(n + 1) * 16]
-        got_r3 = [send(wb3.at[m], r3.at[d], near[d]) for d, m in enumerate(near_ids)]
+        got_r3 = send_all([(wb3.at[m], r3.at[d], near[d]) for d, m in enumerate(near_ids)], r3)
         fts[y] = act
-        got_feat = [send(fts.at[y], fts.at[y], device) for device in y_peers]
+        got_feat = send_all([(fts.at[y], fts.at[y], device) for device in y_peers], fts.at[pl.ds(0, ny - 1)])
 
         arrive(*got_grad)
         row, lane = grid(256, 128)
@@ -368,11 +384,10 @@
                 term = mm_t(columns_two(i, j), g2e[(i + 1) * 3 + j + 1])
                 part = term if part is None else part + term
         wb2[...] = jnp.zeros_like(wb2)
-        for n in range(54):
-            lanes, at = divmod(n * 8, 112)
-            group, at = divmod(at, rows2)
-            wb2[group, at:at + 8, lanes * 32:(lanes + 1) * 32] = part[n * 8:(n + 1) * 8]
-        got_r2 = [send(wb2.at[m], r2.at[d], near[d]) for d, m in enumerate(near_ids)]
+        for n in range(432 // rows2):
+            lanes, at = divmod(n * rows2, 112)
+            wb2[at // rows2, :, lanes * 32:(lanes + 1) * 32] = part[n * rows2:(n + 1) * rows2]
+        got_r2 = send_all([(wb2.at[m], r2.at[d], near[d]) for d, m in enumerate(near_ids)], r2)
 
         for p in range(2):
             rows = g2e[...].reshape(288, 256)[:, p * 128:(p + 1) * 128]
@@ -390,7 +405,7 @@
                 part = term if part is None else part + term
         part = jnp.concatenate([part[t * 16:t * 16 + 12] for t in range(9)] + [jnp.zeros((20, 16), F32)], axis=0)
         y1[near_me] = part.T
-        got_y1 = [send(y1.at[near_me], y1.at[near_me], device) for device in near]
+        got_y1 = send_all([(y1.at[near_me], y1.at[near_me], device) for device in near], y1.at[pl.ds(0, n_near - 1)])
 
         def total(first, refs):
             value = first
@@ -398,41 +413,41 @@
                 value = value + ref
             return value
 
-        arrive(*got_r3)
+        arrive_all(got_r3)
         z3[far_me] = total(wb3[near_me], [r3[d] for d in range(n_near - 1)])
-        got_z3 = [send(z3.at[far_me], z3.at[far_me], device) for device in far]
+        got_z3 = send_all([(z3.at[far_me], z3.at[far_me], device) for device in far], z3.at[pl.ds(0, n_far - 1)])
         row, lane = grid(256, 256)
         swap = marks(((row >> 4) == (lane & 15)) & ((row & 15) == (lane >> 4)))
         block = mm(swap, d1b[...]).astype(BF16)
         for b in range(4):
             gact[b] = block[:, b * 128:(b + 1) * 128]
         store(gact, gact_out)
-        arrive(*got_feat)
+        arrive_all(got_feat)
         feat[...] = mm(jnp.concatenate([fts[k] for k in range(4)], axis=1), regroup).astype(BF16)
         store(feat, feat_out)
-        arrive(*got_r2)
+        arrive_all(got_r2)
         z2[far_me] = total(wb2[near_me], [r2[d] for d in range(n_near - 1)])
-        got_z2 = [send(z2.at[far_me], z2.at[far_me], device) for device in far]
-        arrive(*got_y1)
+        got_z2 = send_all([(z2.at[far_me], z2.at[far_me], device) for device in far], z2.at[pl.ds(0, n_far - 1)])
+        arrive_all(got_y1)
         z1[far_me] = total(y1[0], [y1[m] for m in range(1, n_near)])
-        got_z1 = [send(z1.at[far_me], z1.at[far_me], device) for device in far]
-
-        arrive(*got_z3)
+        got_z1 = send_all([(z1.at[far_me], z1.at[far_me], device) for device in far], z1.at[pl.ds(0, n_far - 1)])
+
+        arrive_all(got_z3)
         f3[near_me] = total(z3[0], [z3[m] for m in range(1, n_far)]) * scales[2]
-        got_f3 = [send(f3.at[near_me], f3.at[near_me], device) for device in near]
-        arrive(*got_z2)
+        got_f3 = send_all([(f3.at[near_me], f3.at[near_me], device) for device in near], f3.at[pl.ds(0, n_near - 1)])
+        arrive_all(got_z2)
         f2[near_me] = total(z2[0], [z2[m] for m in range(1, n_far)]) * scales[1]
-        got_f2 = [send(f2.at[near_me], f2.at[near_me], device) for device in near]
-        arrive(*got_z1)
+        got_f2 = send_all([(f2.at[near_me], f2.at[near_me], device) for device in near], f2.at[pl.ds(0, n_near - 1)])
+        arrive_all(got_z1)
         part = total(z1[0], [z1[m] for m in range(1, n_far)]) * scales[0]
         o1[...] = part.T[:108].reshape(27, 4, 16)
         store(o1, o1_out)
-        arrive(*got_f3)
+        arrive_all(got_f3)
         part = f3[...].reshape(512, 128)[:432]
         for half in range(2):
             o3[half * 432:(half + 1) * 432, :] = part[:, half * 64:(half + 1) * 64]
         store(o3, o3_out)
-        arrive(*got_f2)
+        arrive_all(got_f2)
         part = f2[...].reshape(128, 128)
         for n in range(27):
             lanes, at = divmod(n * 16, 112)
@@ -440,6 +455,8 @@
         store(o2, o2_out)
         for copy in started:
             copy.wait_send()
+        for landed, n in grouped:
+            pltpu.make_async_copy(landed, landed, ss.at[n]).wait()
         for copy in stores:
             copy.wait()
 
@@ -498,7 +515,7 @@
 
 def solution(mesh):
     ny, ns = mesh.shape["sample"], mesh.shape["space"]
-    nx = 4 if ns % 8 == 0 else 2
+    nx = 4 if ns % 8 == 0 else 1
 
     def local(volumes, weight_one, weight_two, weight_three, feature_grad):
         cells = volumes.shape[0] * volumes.shape[2] * ns * volumes.shape[3] * ny * volumes.shape[4]

time: 53.8 us -> 47.4 us (0.88)
  Pallas kernels: 53 us -> 46.6 us
    pallas_call x1, Pallas kernels: 50.8 us -> 44.4 us  [local(): make_kernel(ny, ns, nx, scales)]
where the time goes in v3:
time: 47.4 us; the launch traced here: 47.2 us
  Pallas kernels  46.6 us (98%)
  between operations  0.64 us (1%)
    pallas_call x1, Pallas kernels, local(): make_kernel(ny, ns, nx, scales)  44.4 us
    pallas_call x1, Pallas kernels, local(): pl.pallas_call(hand_over, out_shape=(jax.ShapeDtypeStruct((64, 128), BF16...  2.18 us

profile of v3, /device:TPU:1, one launch (start us, length us, event | category | flops | bytes accessed | tf_op | source)
XLA Modules:
  0.0 47.2 jit_solution(314607022951410727)
XLA Ops:
  0.6 44.4 %layers.1 = (bf16[64,128]{1,0:T(8,128)(2,1)}, bf16[4,256,128]{2,1,0:T(8,128)(2,1)}, f32[27,4,16]{2,1,0:T(4,128)}, f32[432,32]{1,0:T(8,128)}, f32[864,64]{1,0:T(8,128)}) custom-call(bf16[4,256,256]{2,1,0:T(8,128)(2,1)} %bitcast.22, bf16[27,4,16]{2,1,0:T(4,128)(2,1)} %bitcast.29, bf16[432,32]{1,0:T(8,128)(2,1)} %bitcast.27, bf16[864,64]{1,0:T(8,128)(2,1)} %bitcast.25, ...), custom_call_target="tpu_custom_call" | custom-call | flops 3000000000 | bytes 4000000 | tf_op jit(solution)/shard_map/layers/pallas_call | solution.py:527
  45.0 2.2 %hand_over.1 = (bf16[64,128]{1,0:T(8,128)(2,1)}, bf16[4,256,128]{2,1,0:T(8,128)(2,1)}, f32[27,4,16]{2,1,0:T(4,128)}, f32[432,32]{1,0:T(8,128)}, f32[864,64]{1,0:T(8,128)}) custom-call(bf16[64,128]{1,0:T(8,128)(2,1)} %get-tuple-element.15.refs_0_, bf16[4,256,128]{2,1,0:T(8,128)(2,1)} %get-tuple-element.16.refs_1_, f32[27,4,16]{2,1,0:T(4,128)} %get-tuple-element.17.refs_2_, ...), custom_call_target="tpu_custom_call" | custom-call | tf_op jit(solution)/shard_map/hand_over/pallas_call | solution.py:531

commit v4 on v3

--- a/solution.py
+++ b/solution.py
@@ -433,7 +433,7 @@
         got_z1 = send_all([(z1.at[far_me], z1.at[far_me], device) for device in far], z1.at[pl.ds(0, n_far - 1)])
 
         arrive_all(got_z3)
-        f3[near_me] = total(z3[0], [z3[m] for m in range(1, n_far)]) * scales[2]
+        f3[near_me] = (total(z3[0], [z3[m] for m in range(1, n_far)]) * scales[2]).astype(BF16)
         got_f3 = send_all([(f3.at[near_me], f3.at[near_me], device) for device in near], f3.at[pl.ds(0, n_near - 1)])
         arrive_all(got_z2)
         f2[near_me] = total(z2[0], [z2[m] for m in range(1, n_far)]) * scales[1]
@@ -443,7 +443,7 @@
         o1[...] = part.T[:108].reshape(27, 4, 16)
         store(o1, o1_out)
         arrive_all(got_f3)
-        part = f3[...].reshape(512, 128)[:432]
+        part = f3[...].astype(F32).reshape(512, 128)[:432]
         for half in range(2):
             o3[half * 432:(half + 1) * 432, :] = part[:, half * 64:(half + 1) * 64]
         store(o3, o3_out)
@@ -474,7 +474,7 @@
         vm((4, 64, 128), BF16), vm((4, 64, 128), BF16), vm((4, 64, 128), BF16), vm((4, 192, 256), BF16),
         vm((9, 32, 256), BF16), vm((9, 96, 512), BF16), vm((256, 512), BF16),
         vm((n_near, rows3, 128), F32), vm((n_near - 1, rows3, 128), F32), vm((n_far, rows3, 128), F32),
-        vm((n_near, rows3, 128), F32),
+        vm((n_near, rows3, 128), BF16),
         vm((n_near, rows2, 128), F32), vm((n_near - 1, rows2, 128), F32), vm((n_far, rows2, 128), F32),
         vm((n_near, rows2, 128), F32),
         vm((n_near, 16, 128), F32), vm((n_far, 16, 128), F32),
@@ -502,13 +502,23 @@
 
 def hand_over(*refs):
     given, results, held, (sems,) = refs[:5], refs[5:10], refs[10:15], refs[15:]
-    come = [pltpu.make_async_copy(given[n], held[n], sems.at[n]) for n in range(5)]
-    go = [pltpu.make_async_copy(held[n], results[n], sems.at[5 + n]) for n in range(5)]
+    parts = [(n, None) for n in (4, 3, 2, 0)] + [(1, b) for b in range(4)]
+
+    def part(ref, b):
+        return ref if b is None else ref.at[b]
+
+    come = [
+        pltpu.make_async_copy(part(given[n], b), part(held[n], b), sems.at[k]) for k, (n, b) in enumerate(parts)
+    ]
+    go = [
+        pltpu.make_async_copy(part(held[n], b), part(results[n], b), sems.at[8 + k])
+        for k, (n, b) in enumerate(parts)
+    ]
     for copy in come:
         copy.start()
-    for n in (0, 2, 3, 4, 1):
-        come[n].wait()
-        go[n].start()
+    for first, then in zip(come, go):
+        first.wait()
+        then.start()
     for copy in go:
         copy.wait()
 
@@ -541,7 +551,7 @@
             out_specs=[pl.BlockSpec(memory_space=pltpu.HBM)] * 5,
             scratch_shapes=[
                 pltpu.VMEM((64, 128), BF16), pltpu.VMEM((4, 256, 128), BF16), pltpu.VMEM((27, 4, 16), F32),
-                pltpu.VMEM((432, 32), F32), pltpu.VMEM((864, 64), F32), pltpu.SemaphoreType.DMA((10,)),
+                pltpu.VMEM((432, 32), F32), pltpu.VMEM((864, 64), F32), pltpu.SemaphoreType.DMA((16,)),
             ],
             compiler_params=pltpu.CompilerParams(vmem_limit_bytes=63 * 1024 * 1024),
             name="hand_over",

time: 47.4 us -> 47.3 us (level)
  no operation moved by 1% of the time
where the time goes in v4:
time: 47.3 us; the launch traced here: 47.1 us
  Pallas kernels  46.5 us (98%)
  between operations  0.64 us (1%)
    pallas_call x1, Pallas kernels, local(): make_kernel(ny, ns, nx, scales)  44.4 us
    pallas_call x1, Pallas kernels, local(): pl.pallas_call(hand_over, out_shape=(jax.ShapeDtypeStruct((64, 128), BF16...  2.09 us

profile of v4, /device:TPU:1, one launch (start us, length us, event | category | flops | bytes accessed | tf_op | source)
XLA Modules:
  0.0 47.1 jit_solution(8417074182610968622)
XLA Ops:
  0.6 44.4 %layers.1 = (bf16[64,128]{1,0:T(8,128)(2,1)}, bf16[4,256,128]{2,1,0:T(8,128)(2,1)}, f32[27,4,16]{2,1,0:T(4,128)}, f32[432,32]{1,0:T(8,128)}, f32[864,64]{1,0:T(8,128)}) custom-call(bf16[4,256,256]{2,1,0:T(8,128)(2,1)} %bitcast.22, bf16[27,4,16]{2,1,0:T(4,128)(2,1)} %bitcast.29, bf16[432,32]{1,0:T(8,128)(2,1)} %bitcast.27, bf16[864,64]{1,0:T(8,128)(2,1)} %bitcast.25, ...), custom_call_target="tpu_custom_call" | custom-call | flops 3000000000 | bytes 4000000 | tf_op jit(solution)/shard_map/layers/pallas_call | solution.py:537
  45.0 2.1 %hand_over.1 = (bf16[64,128]{1,0:T(8,128)(2,1)}, bf16[4,256,128]{2,1,0:T(8,128)(2,1)}, f32[27,4,16]{2,1,0:T(4,128)}, f32[432,32]{1,0:T(8,128)}, f32[864,64]{1,0:T(8,128)}) custom-call(bf16[64,128]{1,0:T(8,128)(2,1)} %get-tuple-element.15.refs_0_, bf16[4,256,128]{2,1,0:T(8,128)(2,1)} %get-tuple-element.16.refs_1_, f32[27,4,16]{2,1,0:T(4,128)} %get-tuple-element.17.refs_2_, ...), custom_call_target="tpu_custom_call" | custom-call | tf_op jit(solution)/shard_map/hand_over/pallas_call | solution.py:541

commit v5 on v4

--- a/solution.py
+++ b/solution.py
@@ -337,7 +337,7 @@
         got_grad = [send(g3.at[3], g3.at[to], following[i]) for i, to in ((2, 0), (1, 2), (0, 1))]
 
         part = mm_t(columns_three, grad_three)
-        part = jnp.concatenate([part[:432], part[432:]], axis=1)
+        part = jnp.concatenate([part[:432], part[432:]], axis=1).astype(BF16)
         wb3[...] = jnp.zeros_like(wb3)
         for n in range(27):
             group, at = divmod(n * 16, rows3)
@@ -404,13 +404,13 @@
                 term = mm_t(columns_one(i, j), grad_one)
                 part = term if part is None else part + term
         part = jnp.concatenate([part[t * 16:t * 16 + 12] for t in range(9)] + [jnp.zeros((20, 16), F32)], axis=0)
-        y1[near_me] = part.T
+        y1[near_me] = part.T.astype(BF16)
         got_y1 = send_all([(y1.at[near_me], y1.at[near_me], device) for device in near], y1.at[pl.ds(0, n_near - 1)])
 
         def total(first, refs):
-            value = first
+            value = first.astype(F32)
             for ref in refs:
-                value = value + ref
+                value = value + ref.astype(F32)
             return value
 
         arrive_all(got_r3)
@@ -473,11 +473,11 @@
         vm((3, 3, 32, 256), BF16), vm((3, 3, 32, 256), BF16), vm((3, 3, 96, 128), BF16),
         vm((4, 64, 128), BF16), vm((4, 64, 128), BF16), vm((4, 64, 128), BF16), vm((4, 192, 256), BF16),
         vm((9, 32, 256), BF16), vm((9, 96, 512), BF16), vm((256, 512), BF16),
-        vm((n_near, rows3, 128), F32), vm((n_near - 1, rows3, 128), F32), vm((n_far, rows3, 128), F32),
+        vm((n_near, rows3, 128), BF16), vm((n_near - 1, rows3, 128), BF16), vm((n_far, rows3, 128), F32),
         vm((n_near, rows3, 128), BF16),
         vm((n_near, rows2, 128), F32), vm((n_near - 1, rows2, 128), F32), vm((n_far, rows2, 128), F32),
         vm((n_near, rows2, 128), F32),
-        vm((n_near, 16, 128), F32), vm((n_far, 16, 128), F32),
+        vm((n_near, 16, 128), BF16), vm((n_far, 16, 128), F32),
         pltpu.SemaphoreType.DMA((COPIES,)), pltpu.SemaphoreType.DMA((COPIES,)),
     ]
     return pl.pallas_call(

time: 47.3 us -> 47.2 us (level)
  no operation moved by 1% of the time
where the time goes in v5:
time: 47.2 us; the launch traced here: 47 us
  Pallas kernels  46.4 us (98%)
  between operations  0.64 us (1%)
    pallas_call x1, Pallas kernels, local(): make_kernel(ny, ns, nx, scales)  44.3 us
    pallas_call x1, Pallas kernels, local(): pl.pallas_call(hand_over, out_shape=(jax.ShapeDtypeStruct((64, 128), BF16...  2.09 us

profile of v5, /device:TPU:1, one launch (start us, length us, event | category | flops | bytes accessed | tf_op | source)
XLA Modules:
  0.0 47.0 jit_solution(17012728181683253479)
XLA Ops:
  0.6 44.3 %layers.1 = (bf16[64,128]{1,0:T(8,128)(2,1)}, bf16[4,256,128]{2,1,0:T(8,128)(2,1)}, f32[27,4,16]{2,1,0:T(4,128)}, f32[432,32]{1,0:T(8,128)}, f32[864,64]{1,0:T(8,128)}) custom-call(bf16[4,256,256]{2,1,0:T(8,128)(2,1)} %bitcast.22, bf16[27,4,16]{2,1,0:T(4,128)(2,1)} %bitcast.29, bf16[432,32]{1,0:T(8,128)(2,1)} %bitcast.27, bf16[864,64]{1,0:T(8,128)(2,1)} %bitcast.25, ...), custom_call_target="tpu_custom_call" | custom-call | flops 3000000000 | bytes 4000000 | tf_op jit(solution)/shard_map/layers/pallas_call | solution.py:537
  44.9 2.1 %hand_over.1 = (bf16[64,128]{1,0:T(8,128)(2,1)}, bf16[4,256,128]{2,1,0:T(8,128)(2,1)}, f32[27,4,16]{2,1,0:T(4,128)}, f32[432,32]{1,0:T(8,128)}, f32[864,64]{1,0:T(8,128)}) custom-call(bf16[64,128]{1,0:T(8,128)(2,1)} %get-tuple-element.15.refs_0_, bf16[4,256,128]{2,1,0:T(8,128)(2,1)} %get-tuple-element.16.refs_1_, f32[27,4,16]{2,1,0:T(4,128)} %get-tuple-element.17.refs_2_, ...), custom_call_target="tpu_custom_call" | custom-call | tf_op jit(solution)/shard_map/hand_over/pallas_call | solution.py:541

commit v6 on v5

--- a/solution.py
+++ b/solution.py
@@ -54,7 +54,7 @@
     rows3, rows2 = 512 // n_near, 128 // n_near
 
     def kernel(vol_in, w1t_in, w2t_in, w3t_in, fg_in, feat_out, gact_out, o1_out, o2_out, o3_out,
-               vol, w1t, w2t, w3t, fg, ls, feat, gact, o1, o2, o3, os,
+               vol, w1t, w2t, w3t, fg, ls, feat, gact, o1, os,
                s1, s2, s3, pm, w1, w2, w3, w2k, w3k, hs, hr, vsm, e1, a1, sl1, e2, a2, sl2, e3, fgs, fts,
                g3, gg3, g2e, gg2, d1b, wb3, r3, z3, f3, wb2, r2, z2, f2, y1, z1, ss, rs):
         y = lax.axis_index("sample")
@@ -443,16 +443,9 @@
         o1[...] = part.T[:108].reshape(27, 4, 16)
         store(o1, o1_out)
         arrive_all(got_f3)
-        part = f3[...].astype(F32).reshape(512, 128)[:432]
-        for half in range(2):
-            o3[half * 432:(half + 1) * 432, :] = part[:, half * 64:(half + 1) * 64]
-        store(o3, o3_out)
+        store(f3, o3_out)
         arrive_all(got_f2)
-        part = f2[...].reshape(128, 128)
-        for n in range(27):
-            lanes, at = divmod(n * 16, 112)
-            o2[n * 16:(n + 1) * 16, :] = part[at:at + 16, lanes * 32:(lanes + 1) * 32]
-        store(o2, o2_out)
+        store(f2, o2_out)
         for copy in started:
             copy.wait_send()
         for landed, n in grouped:
@@ -464,7 +457,7 @@
     scratch = [
         vm((4, 256, 256), BF16), vm((27, 4, 16), BF16), vm((432, 32), BF16), vm((864, 64), BF16), vm((64, 128), BF16),
         pltpu.SemaphoreType.DMA((5,)),
-        vm((64, 128), BF16), vm((4, 256, 128), BF16), vm((27, 4, 16), F32), vm((432, 32), F32), vm((864, 64), F32),
+        vm((64, 128), BF16), vm((4, 256, 128), BF16), vm((27, 4, 16), F32),
         pltpu.SemaphoreType.DMA((5,)),
         vm((256, 384), BF16), vm((256, 384), BF16), vm((256, 384), BF16), vm((128, 96), BF16),
         vm((16, 144), BF16), vm((32, 432), BF16), vm((64, 864), BF16), vm((144, 96), BF16), vm((288, 192), BF16),
@@ -486,8 +479,8 @@
             jax.ShapeDtypeStruct((64, 128), BF16),
             jax.ShapeDtypeStruct((4, 256, 128), BF16),
             jax.ShapeDtypeStruct((27, 4, 16), F32),
-            jax.ShapeDtypeStruct((432, 32), F32),
-            jax.ShapeDtypeStruct((864, 64), F32),
+            jax.ShapeDtypeStruct((n_near, rows2, 128), F32),
+            jax.ShapeDtypeStruct((n_near, rows3, 128), BF16),
         ),
         in_specs=[pl.BlockSpec(memory_space=pltpu.HBM)] * 5,
         out_specs=[pl.BlockSpec(memory_space=pltpu.HBM)] * 5,
@@ -501,8 +494,9 @@
 
 
 def hand_over(*refs):
-    given, results, held, (sems,) = refs[:5], refs[5:10], refs[10:15], refs[15:]
-    parts = [(n, None) for n in (4, 3, 2, 0)] + [(1, b) for b in range(4)]
+    given, results, held = refs[:5], refs[5:10], refs[10:15]
+    two, three, sems = refs[15:]
+    parts = [(4, None), (3, None), (2, None), (0, None)] + [(1, b) for b in range(4)]
 
     def part(ref, b):
         return ref if b is None else ref.at[b]
@@ -510,15 +504,27 @@
     come = [
         pltpu.make_async_copy(part(given[n], b), part(held[n], b), sems.at[k]) for k, (n, b) in enumerate(parts)
     ]
+    source = {0: held[0], 1: held[1], 2: held[2], 3: two, 4: three}
     go = [
-        pltpu.make_async_copy(part(held[n], b), part(results[n], b), sems.at[8 + k])
+        pltpu.make_async_copy(part(source[n], b), part(results[n], b), sems.at[8 + k])
         for k, (n, b) in enumerate(parts)
     ]
     for copy in come:
         copy.start()
-    for first, then in zip(come, go):
-        first.wait()
-        then.start()
+    for k in range(2, 8):
+        come[k].wait()
+        go[k].start()
+    come[0].wait()
+    packed = held[4][...].astype(F32).reshape(512, 128)[:432]
+    for half in range(2):
+        three[half * 432:(half + 1) * 432, :] = packed[:, half * 64:(half + 1) * 64]
+    go[0].start()
+    come[1].wait()
+    packed = held[3][...].reshape(128, 128)
+    for n in range(27):
+        lanes, at = divmod(n * 16, 112)
+        two[n * 16:(n + 1) * 16, :] = packed[at:at + 16, lanes * 32:(lanes + 1) * 32]
+    go[1].start()
     for copy in go:
         copy.wait()
 
@@ -551,6 +557,7 @@
             out_specs=[pl.BlockSpec(memory_space=pltpu.HBM)] * 5,
             scratch_shapes=[
                 pltpu.VMEM((64, 128), BF16), pltpu.VMEM((4, 256, 128), BF16), pltpu.VMEM((27, 4, 16), F32),
+                pltpu.VMEM(two.shape, F32), pltpu.VMEM(three.shape, BF16),
                 pltpu.VMEM((432, 32), F32), pltpu.VMEM((864, 64), F32), pltpu.SemaphoreType.DMA((16,)),
             ],
             compiler_params=pltpu.CompilerParams(vmem_limit_bytes=63 * 1024 * 1024),

time: 47.2 us -> 47.1 us (level)
  no operation moved by 1% of the time
where the time goes in v6:
time: 47.1 us; the launch traced here: 46.9 us
  Pallas kernels  46.3 us (98%)
  between operations  0.64 us (1%)
    pallas_call x1, Pallas kernels, local(): make_kernel(ny, ns, nx, scales)  44.1 us
    pallas_call x1, Pallas kernels, local(): pl.pallas_call(hand_over, out_shape=(jax.ShapeDtypeStruct((64, 128), BF16...  2.15 us

profile of v6, /device:TPU:1, one launch (start us, length us, event | category | flops | bytes accessed | tf_op | source)
XLA Modules:
  0.0 46.9 jit_solution(6908968022264026148)
XLA Ops:
  0.6 44.1 %layers.1 = (bf16[64,128]{1,0:T(8,128)(2,1)}, bf16[4,256,128]{2,1,0:T(8,128)(2,1)}, f32[27,4,16]{2,1,0:T(4,128)}, f32[32,4,128]{2,1,0:T(4,128)}, bf16[32,16,128]{2,1,0:T(8,128)(2,1)}) custom-call(bf16[4,256,256]{2,1,0:T(8,128)(2,1)} %bitcast.22, bf16[27,4,16]{2,1,0:T(4,128)(2,1)} %bitcast.29, bf16[432,32]{1,0:T(8,128)(2,1)} %bitcast.27, ...), custom_call_target="tpu_custom_call" | custom-call | flops 3000000000 | bytes 4000000 | tf_op jit(solution)/shard_map/layers/pallas_call | solution.py:543
  44.8 2.2 %hand_over.1 = (bf16[64,128]{1,0:T(8,128)(2,1)}, bf16[4,256,128]{2,1,0:T(8,128)(2,1)}, f32[27,4,16]{2,1,0:T(4,128)}, f32[432,32]{1,0:T(8,128)}, f32[864,64]{1,0:T(8,128)}) custom-call(bf16[64,128]{1,0:T(8,128)(2,1)} %get-tuple-element.15.refs_0_, bf16[4,256,128]{2,1,0:T(8,128)(2,1)} %get-tuple-element.16.refs_1_, f32[27,4,16]{2,1,0:T(4,128)} %get-tuple-element.17.refs_2_, ...), custom_call_target="tpu_custom_call" | custom-call | tf_op jit(solution)/shard_map/hand_over/pallas_call | solution.py:547
